TPU v7x, 32 devices: a whole 2x2x4 slice. The times are simulated.
32 devices in a mesh: dp: 4 (over y, x), expert: 8 (over z, core).
Axes of the slice: x: 2, y: 2, z: 4, core: 2. Of those that a mesh axis runs over, the one named last changes fastest.
Arguments:
- out_grad: bfloat16 [4, 1024, 4096], P('dp', 'expert'), may hold values from -6 to 6
- count: int32 [4, 1024], P('dp', 'expert'), may hold values from 0 to 8, as said below
- chosen: int32 [4, 16, 128], P('dp', 'expert'), may hold values from 0 to 1023, as said below
- gates: float32 [4, 16, 128], P('dp', 'expert'), may hold values from 0.1 to 1
- x_slots: bfloat16 [4, 16, 128, 4096], P('dp', 'expert'), may hold values from -6 to 6
- w_in: bfloat16 [16, 4096, 512], P('expert', None, 'dp'), may hold values from -0.09375 to 0.09375
- w_out: bfloat16 [16, 512, 4096], P('expert', 'dp'), may hold values from -0.25 to 0.25
Outputs:
- token_grad: bfloat16 [4, 1024, 4096], P('dp', 'expert')
- gate_grad: float32 [4, 16, 128], P('dp', 'expert')
- w_in_grad: bfloat16 [16, 4096, 512], P('expert', None, 'dp')
- w_out_grad: bfloat16 [16, 512, 4096], P('expert', 'dp')
Inputs may be any that keep to these rules, and one draw needn't show every extreme that they name: `chosen`: in each group, one expert's 128 slots name different tokens, and one device's 2 experts together name different tokens. Within a group, the slots of one device's experts name at most 48 tokens of any one device (device j of expert holds the group's tokens j * 128 to (j + 1) * 128 - 1), and every such device's experts name exactly 48 tokens of some device. count[g,t] is the number of slots of group g, over all experts, whose chosen token is t; each device of expert contributes at most one.
All inputs are finite; a program needn't handle non-finite values.
Results may differ from a plain program's by a relative error of at most 0.007.
Values may be sent and summed in bfloat16 or wider, within the bound.
A program may use at most 128 MiB of HBM per device.

v0:
```python
import jax
import jax.numpy as jnp
from jax import lax
from jax.sharding import PartitionSpec as P

SQRT_HALF = 0.7071067811865476
INV_ROOT_TWO_PI = 0.3989422804014327


def expert_terms(inputs, upstream, scale_w, count_f, proj_in, proj_out):
    pre = jnp.einsum("gecd,edf->gecf", inputs, proj_in, preferred_element_type=jnp.float32)
    normal_cdf = 0.5 * (1.0 + lax.erf(pre * SQRT_HALF))
    slope = normal_cdf + pre * jnp.exp(-0.5 * pre * pre) * INV_ROOT_TWO_PI
    hidden = (pre * normal_cdf).astype(jnp.bfloat16)
    project = jnp.einsum("gecd,efd->gecf", upstream, proj_out, preferred_element_type=jnp.float32)
    gate_part = jnp.sum(hidden.astype(jnp.float32) * project, axis=3) / count_f
    pre_grad = (scale_w[..., None] * project * slope).astype(jnp.bfloat16)
    out_slot = (scale_w[..., None] * upstream.astype(jnp.float32)).astype(jnp.bfloat16)
    back_part = jnp.einsum("gecf,edf->gecd", pre_grad, proj_in, preferred_element_type=jnp.float32)
    grad_in = jnp.einsum("gecd,gecf->gedf", inputs, pre_grad, preferred_element_type=jnp.float32)
    grad_out = jnp.einsum("gecf,gecd->gefd", hidden, out_slot, preferred_element_type=jnp.float32)
    return (back_part, gate_part, grad_in, grad_out)


def shards(out_grad, count, chosen, gates, x_slots, w_in, w_out):
    tok_rows = out_grad.shape[1]
    width = out_grad.shape[2]
    local_experts = chosen.shape[1]
    capacity = chosen.shape[2]
    slots = local_experts * capacity
    owners = lax.axis_size("expert")
    per_peer = 3 * tok_rows // owners
    token_ids = chosen.reshape(slots)
    source = token_ids // tok_rows
    local_row = token_ids % tok_rows
    onehot = (source[:, None] == jnp.arange(owners, dtype=jnp.int32)[None, :]).astype(jnp.int32)
    slot_rank = jnp.sum((jnp.cumsum(onehot, axis=0) - onehot) * onehot, axis=1)
    slot_place = source * per_peer + slot_rank
    request = jnp.full((owners * per_peer,), -1, jnp.int32).at[slot_place].set(local_row)
    asked_rows = lax.all_to_all(
        request.reshape(owners, per_peer), "expert", split_axis=0, concat_axis=0, tiled=True
    )
    is_valid = asked_rows >= 0
    safe_rows = jnp.where(is_valid, asked_rows, 0)
    sent_rows = jnp.where(is_valid[..., None], out_grad[0][safe_rows], 0)
    sent_counts = jnp.where(is_valid, count[0][safe_rows], 1).astype(jnp.bfloat16)
    got_rows, got_counts = (
        lax.all_to_all(sent_rows, "expert", split_axis=0, concat_axis=0, tiled=True),
        lax.all_to_all(sent_counts, "expert", split_axis=0, concat_axis=0, tiled=True),
    )
    slot_grad = got_rows.reshape(owners * per_peer, width)[slot_place]
    slot_count = got_counts.reshape(owners * per_peer)[slot_place].astype(jnp.float32)
    slot_scale = gates.reshape(slots) / slot_count
    inputs = x_slots.reshape(slots, width)
    groups = lax.axis_size("dp")
    all_inputs, all_grad = (
        lax.all_gather(inputs, "dp", axis=0, tiled=True),
        lax.all_gather(slot_grad, "dp", axis=0, tiled=True),
    )
    all_scales = lax.all_gather(jnp.stack([slot_scale, slot_count]), "dp", axis=1, tiled=True)
    back_part, gate_part, grad_in, grad_out = expert_terms(
        all_inputs.reshape(groups, local_experts, capacity, width),
        all_grad.reshape(groups, local_experts, capacity, width),
        all_scales[0].reshape(groups, local_experts, capacity),
        all_scales[1].reshape(groups, local_experts, capacity),
        w_in,
        w_out,
    )
    rounded_in = lax.optimization_barrier(grad_in.astype(jnp.bfloat16)).astype(jnp.float32)
    rounded_out = lax.optimization_barrier(grad_out.astype(jnp.bfloat16)).astype(jnp.float32)
    w_in_grad = jnp.sum(rounded_in, axis=0).astype(jnp.bfloat16)
    w_out_grad = jnp.sum(rounded_out, axis=0).astype(jnp.bfloat16)
    back_own, gate_own = (
        lax.psum_scatter(
            back_part.reshape(groups * slots, width), "dp", scatter_dimension=0, tiled=True
        ),
        lax.psum_scatter(gate_part.reshape(groups * slots), "dp", scatter_dimension=0, tiled=True),
    )
    slot_back = back_own.astype(jnp.bfloat16)
    outgoing = jnp.zeros((owners * per_peer, width), jnp.bfloat16).at[slot_place].set(slot_back)
    returned = lax.all_to_all(
        outgoing.reshape(owners, per_peer, width), "expert", split_axis=0, concat_axis=0, tiled=True
    )
    target = jnp.where(is_valid, asked_rows, tok_rows).reshape(-1)
    token_sum = (
        jnp.zeros((tok_rows, width), jnp.float32)
        .at[target]
        .add(returned.reshape(owners * per_peer, width).astype(jnp.float32), mode="drop")
    )
    token_grad = token_sum.astype(jnp.bfloat16)[None]
    gate_grad = gate_own.reshape(1, local_experts, capacity)
    return (token_grad, gate_grad, w_in_grad, w_out_grad)


def solution(mesh):
    return jax.shard_map(
        shards,
        mesh=mesh,
        in_specs=(
            P("dp", "expert", None),
            P("dp", "expert"),
            P("dp", "expert", None),
            P("dp", "expert", None),
            P("dp", "expert", None, None),
            P("expert", None, "dp"),
            P("expert", "dp", None),
        ),
        out_specs=(
            P("dp", "expert", None),
            P("dp", "expert", None),
            P("expert", None, "dp"),
            P("expert", "dp", None),
        ),
        check_vma=False,
    )
```

profile of v0, /device:TPU:0, one launch (start us, length us, event | category | flops | bytes accessed | tf_op | source)
XLA Modules:
  0.0 480.0 jit_solution(8285078968793667848)
XLA Ops:
  7.2 0.7 all-gather.4.cloned.1.call-update
  7.9 0.7 and_select_fusion.2
  9.5 0.7 and_select_fusion.1
  10.3 0.7 compare_select_fusion.4
  10.9 1.4 scatter_custom_fusion
  12.4 11.7 %all_to_all.31 = s32[8,1,48]{2,1,0:T(1,128)S(1)} all-to-all(s32[8,1,48]{2,1,0:T(1,128)S(1)} %all_to_all.20), channel_id=1, replica_groups=mesh['dp'=4,'expert'=8] {'expert'}, dimensions={0} | all-to-all | bytes 3072 | tf_op jit(solution)/shard_map/all_to_all | solution.py:40
  24.2 2.7 gather_fusion
  27.0 4.1 gather_fusion.2
  31.1 3.8 broadcast_select_fusion
  34.9 4.4 all-to-all-start.2
  39.4 71.5 %all-to-all-done.2 = bf16[8,48,4096]{2,1,0:T(8,128)(2,1)} async-done(((bf16[8,48,4096]{2,1,0:T(8,128)(2,1)}), bf16[8,48,4096]{2,1,0:T(8,128)(2,1)}, u32[]{:S(2)}, u32[]{:S(2)}) %all-to-all-start.2) | async-done | bytes 3145760 | tf_op jit(solution)/shard_map/all_to_all | solution.py:48
  110.9 7.5 %gather_fusion.3 = bf16[256,4096]{1,0:T(8,128)(2,1)} fusion(bf16[384,4096]{1,0:T(8,128)(2,1)} %bitcast.16, s32[1024]{0:T(1024)S(1)} %pad_clamp_fusion), kind=kCustom, calls=%fused_computation.3 | custom fusion | bytes 4195328 | tf_op jit(solution)/shard_map/gather | solution.py:51
  118.5 7.9 %all_to_all.32 = bf16[8,1,48]{2,1,0:T(2,128)(2,1)S(1)} all-to-all(bf16[8,1,48]{2,1,0:T(2,128)(2,1)S(1)} %copy.35), channel_id=1, replica_groups=mesh['dp'=4,'expert'=8] {'expert'}, dimensions={0} | all-to-all | bytes 1536 | tf_op jit(solution)/shard_map/all_to_all | solution.py:49
  126.5 1.9 gather_fusion.1
  128.5 8.3 %all_gather.9 = f32[2,1024]{1,0:T(2,128)S(1)} all-gather(f32[2,256]{1,0:T(2,128)S(1)} %pad_maximum_fusion), channel_id=1, replica_groups=mesh['dp'=4,'expert'=8] {'dp'}, dimensions={1}, use_global_device_ids=true | all-gather | bytes 10240 | tf_op jit(solution)/shard_map/all_gather | solution.py:60
  136.8 7.1 %fusion.20 = f32[4,2,128,128]{2,3,0,1:T(8,128)} fusion(bf16[4,2,128,4096]{3,2,1,0:T(8,128)(2,1)} %bitcast.105, bf16[2,4096,128]{2,1,0:T(8,128)(2,1)S(1)} %copy-done), kind=kOutput, calls=%fused_computation.27 | convolution fusion | flops 1073741824 | bytes 11010048 | tf_op jit(solution)/shard_map/gecd,edf->gecf/dot_general | solution.py:11
  143.9 61.2 %all-gather.6.cloned.1.call-done = bf16[1024,4096]{1,0:T(8,128)(2,1)} async-done(((bf16[256,4096]{1,0:T(8,128)(2,1)}), bf16[1024,4096]{1,0:T(8,128)(2,1)}) %all-gather.6.cloned.1.call-update) | async-done | bytes 8388624 | tf_op jit(solution)/shard_map/all_gather | solution.py:58
  205.1 7.1 %multiply_reduce_fusion = (f32[4,2,128]{2,0,1:T(4,128)S(1)}, bf16[4,2,128,128]{2,3,0,1:T(8,128)(2,1)S(1)}, bf16[4,2,128,128]{2,3,0,1:T(8,128)(2,1)S(1)}) fusion(f32[4,2,128,128]{2,3,0,1:T(8,128)} %fusion.20, f32[4,2,128]{2,0,1:T(4,128)S(1)} %copy.36, bf16[2,128,4096]{2,1,0:T(8,128)(2,1)} %param.13, bf16[4,2,128,4096]{3,2,1,0:T(8,128)(2,1)} %bitcast.103), kind=kOutput, calls=%fused_computation.37 | convolution fusion | flops 1075837952 | bytes 11542528 | tf_op jit(solution)/shard_map/gecd,efd->gecf/dot_general | solution.py:15
  212.2 2.4 convolution_bitcast_fusion
  214.6 6.0 %copy.41 = f32[4,2,128,4096]{3,2,1,0:T(8,128)} copy(f32[4,2,128,4096]{3,2,0,1:T(8,128)S(1)} %convolution_bitcast_fusion) | data formatting | bytes 33554432 | tf_op jit(solution)/shard_map/gecf,edf->gecd/transpose | solution.py:19
  220.7 154.0 %reduce-scatter.2.cloned.1.call-done = f32[256,4096]{1,0:T(8,128)} async-done(((f32[1024,4096]{1,0:T(8,128)}), f32[256,4096]{1,0:T(8,128)}) %reduce-scatter.2.cloned.1.call-update) | async-done | bytes 4194320 | tf_op jit(solution)/shard_map/reduce_scatter | solution.py:74
  374.7 7.2 %scatter_custom_fusion.1 = bf16[384,4096]{1,0:T(8,128)(2,1)} fusion(s32[256]{0:T(256)S(1)} %bitcast.117, f32[256,4096]{1,0:T(8,128)} %reduce-scatter.2.cloned.1.call-done, bf16[]{:T(256)} %constant.56.clone.1), kind=kCustom, calls=%fused_computation.23 | custom fusion | flops 1048576 | bytes 7340034 | tf_op jit(solution)/shard_map/scatter | solution.py:80
  381.9 5.0 %all-to-all-start.3 = ((bf16[8,48,4096]{2,1,0:T(8,128)(2,1)}), bf16[8,48,4096]{2,1,0:T(8,128)(2,1)}, u32[]{:S(2)}, u32[]{:S(2)}) async-start(bf16[8,48,4096]{2,1,0:T(8,128)(2,1)} %bitcast.101), calls=%async_computation.4 | async-start | bytes 6291456 | tf_op jit(solution)/shard_map/all_to_all | solution.py:81
  389.4 8.9 %convert_bitcast_fusion = bf16[4,2,4096,128]{2,3,1,0:T(8,128)(2,1)} fusion(bf16[4,2,128,4096]{3,2,1,0:T(8,128)(2,1)} %bitcast.106, bf16[4,2,128,128]{2,3,0,1:T(8,128)(2,1)S(1)} %get-tuple-element.16), kind=kOutput, calls=%fused_computation.15 | convolution fusion | flops 1077936128 | bytes 17039360 | tf_op jit(solution)/shard_map/gecd,gecf->gedf/dot_general | solution.py:20
  398.4 5.2 %reduce_sum.50 = bf16[2,4096,128]{1,2,0:T(8,128)(2,1)S(1)} reduce(bf16[4,2,4096,128]{2,3,1,0:T(8,128)(2,1)} %convert_bitcast_fusion, bf16[]{:T(256)} %constant.56.clone.1), dimensions={0}, to_apply=%region_9.10 | reduce | flops 3145728 | bytes 10485762 | tf_op jit(solution)/shard_map/reduce_sum | solution.py:71
  403.6 2.5 copy.45
  406.0 9.0 %fusion.6 = bf16[4,2,128,4096]{3,2,1,0:T(8,128)(2,1)} fusion(bf16[4,2,128,4096]{3,2,1,0:T(8,128)(2,1)} %bitcast.104, f32[4,2,128]{2,1,0:T(2,128)S(1)} %bitcast.111, bf16[4,2,128,128]{2,3,0,1:T(8,128)(2,1)S(1)} %get-tuple-element.13), kind=kOutput, calls=%fused_computation.16 | convolution fusion | flops 1090519040 | bytes 17043456 | tf_op jit(solution)/shard_map/gecf,gecd->gefd/dot_general | solution.py:21
  415.0 6.9 %reduce_sum.51 = bf16[2,128,4096]{2,1,0:T(8,128)(2,1)} reduce(bf16[4,2,128,4096]{3,2,1,0:T(8,128)(2,1)} %fusion.6, bf16[]{:T(256)} %constant.56.clone.1), dimensions={0}, to_apply=%region_10.11 | reduce | flops 3145728 | bytes 10485762 | tf_op jit(solution)/shard_map/reduce_sum | solution.py:72
  421.9 9.1 %all-reduce = f32[1024]{0:T(1024)S(1)} all-reduce(f32[1024]{0:T(1024)S(1)} %div.55), channel_id=4, replica_groups=mesh['dp'=4,'expert'=8] {'dp'}, use_global_device_ids=true, to_apply=%region_8.9.clone | all-reduce | flops 1024 | bytes 8192
  431.7 26.8 %all-to-all-done.3 = bf16[8,48,4096]{2,1,0:T(8,128)(2,1)} async-done(((bf16[8,48,4096]{2,1,0:T(8,128)(2,1)}), bf16[8,48,4096]{2,1,0:T(8,128)(2,1)}, u32[]{:S(2)}, u32[]{:S(2)}) %all-to-all-start.3) | async-done | bytes 3145760 | tf_op jit(solution)/shard_map/all_to_all | solution.py:81
  458.5 11.8 %scatter_custom_fusion.2 = f32[128,4096]{1,0:T(8,128)} fusion(s32[384]{0:T(512)S(1)} %fusion.37, bf16[384,4096]{1,0:T(8,128)(2,1)} %bitcast.40, f32[]{:T(128)} %constant.24.clone.1), kind=kCustom, calls=%fused_computation.17 | custom fusion | flops 3145728 | bytes 5242884 | tf_op jit(solution)/shard_map/scatter-add | solution.py:88
  470.3 2.7 convert_bitcast_fusion.1
  (47 shorter events, 4.1 us)
Async XLA Ops:
  7.2 129.7 %copy-start = (bf16[2,4096,128]{2,1,0:T(8,128)(2,1)S(1)}, bf16[2,4096,128]{2,1,0:T(8,128)(2,1)}, u32[]{:S(2)}) copy-start(bf16[2,4096,128]{2,1,0:T(8,128)(2,1)} %param.12) | copy-start | bytes 6291460
  7.2 17.0 %copy-start.2 = (s32[1,128]{1,0:T(1,128)S(1)}, s32[1,128]{1,0:T(1,128)}, u32[]{:S(2)}) copy-start(s32[1,128]{1,0:T(1,128)} %param.8) | copy-start | bytes 1540
  7.2 129.6 %all-gather.4.cloned.1.call-start = ((), (), s32[]{:S(2)}) async-start(), calls=%async_computation.5 | async-start | bytes 10485760 | tf_op jit(solution)/shard_map/all_gather | solution.py:57
  7.2 19.8 %copy-start.3 = (bf16[1,128,4096]{2,1,0:T(8,128)(2,1)S(1)}, bf16[1,128,4096]{2,1,0:T(8,128)(2,1)}, u32[]{:S(2)}) copy-start(bf16[1,128,4096]{2,1,0:T(8,128)(2,1)} %param.7) | copy-start | bytes 3145732
  34.9 76.0 %all-to-all-start.2 = ((bf16[8,48,4096]{2,1,0:T(8,128)(2,1)}), bf16[8,48,4096]{2,1,0:T(8,128)(2,1)}, u32[]{:S(2)}, u32[]{:S(2)}) async-start(bf16[8,48,4096]{2,1,0:T(8,128)(2,1)} %broadcast_select_fusion), calls=%async_computation.2 | async-start | bytes 6291456 | tf_op jit(solution)/shard_map/all_to_all | solution.py:48
  39.4 165.8 %all-gather.6.cloned.1.call-start = ((), (), s32[]{:S(2)}) async-start(), calls=%async_computation.7 | async-start | bytes 10485760 | tf_op jit(solution)/shard_map/all_gather | solution.py:58
  110.9 17.6 %copy-start.4 = (f32[1,2,128]{2,1,0:T(2,128)S(1)}, f32[1,2,128]{2,1,0:T(2,128)}, u32[]{:S(2)}) copy-start(f32[1,2,128]{2,1,0:T(2,128)} %param.10) | copy-start | bytes 3076
  118.4 256.3 %reduce-scatter.2.cloned.1.call-start = ((), (), s32[]{:S(2)}) async-start(), calls=%async_computation.6 | async-start | bytes 20971520 | tf_op jit(solution)/shard_map/reduce_scatter | solution.py:74
  381.9 5.0 %copy-start.5 = (u32[32]{0:T(128)S(1)}, u32[32]{0:T(128)}, u32[]{:S(2)}) copy-start(u32[32]{0:T(128)} %constant.71) | copy-start | bytes 388
  381.9 76.6 %all-to-all-start.3 = ((bf16[8,48,4096]{2,1,0:T(8,128)(2,1)}), bf16[8,48,4096]{2,1,0:T(8,128)(2,1)}, u32[]{:S(2)}, u32[]{:S(2)}) async-start(bf16[8,48,4096]{2,1,0:T(8,128)(2,1)} %bitcast.101), calls=%async_computation.4 | async-start | bytes 6291456 | tf_op jit(solution)/shard_map/all_to_all | solution.py:81
  458.5 14.5 %copy-start.1 = (bf16[2,4096,128]{2,1,0:T(8,128)(2,1)S(1)}, bf16[2,4096,128]{2,1,0:T(8,128)(2,1)}, u32[]{:S(2)}) copy-start(bf16[2,4096,128]{2,1,0:T(8,128)(2,1)} %param.12) | copy-start | bytes 6291460
Sparse Core Ops, SparseCore 0:
  9.9 90.2 all-gather.3
  118.5 86.5 all-gather.5
  220.8 153.8 reduce-scatter.1
where the time goes:
time: 487 us; the launch traced here: 480 us
  waiting for transfers between devices  314 us (64%)
  other arithmetic  41.1 us (8%)
  blocking collectives  37 us (8%)
  matrix products  34.5 us (7%)
  local copies, waits for them, and re-layouts  28.5 us (6%)
  between operations  15 us (3%)
  starting transfers between devices  9.57 us (2%)
    reduce_scatter x1, waiting for transfers between devices, shards(): lax.psum_scatter(back_part.reshape(groups * slots, width), 'dp', scatter_...  154 us
    all_to_all x1, waiting for transfers between devices, shards(): lax.all_to_all(sent_rows, 'expert', split_axis=0, concat_axis=0, tiled=True)  71.5 us
    all_gather x1, waiting for transfers between devices, shards(): lax.all_gather(slot_grad, 'dp', axis=0, tiled=True)  61.2 us
    all_to_all x1, waiting for transfers between devices, shards(): lax.all_to_all(outgoing.reshape(owners, per_peer, width), 'expert', split...  26.8 us
    scatter-add x1, other arithmetic, shards(): token_sum = jnp.zeros((tok_rows, width), jnp.float32).at[target].add(retu...  11.8 us
    all_to_all x1, blocking collectives, shards(): lax.all_to_all(request.reshape(owners, per_peer), 'expert', split_axis=0,...  11.7 us
  transfers between devices with their start and end apart: 5, of which 4 were waited for; matrix products, arithmetic and copies ran while one was open for 14% of the time, Pallas kernels for 0%

commit v1 on v0

v1 whole, which is shorter than its diff:
```python
import jax
import jax.numpy as jnp
from jax import lax
from jax.sharding import PartitionSpec as P

SQRT_HALF = 0.7071067811865476
INV_ROOT_TWO_PI = 0.3989422804014327
BF16 = jnp.bfloat16
F32 = jnp.float32


def swap(value, bit):
    size = lax.axis_size("dp")
    return lax.ppermute(value, "dp", [(i, i ^ bit) for i in range(size)])


def running_rank(mask):
    n = mask.shape[-1]
    before = (jnp.arange(n)[:, None] < jnp.arange(n)[None, :]).astype(BF16)
    ranks = jnp.dot(mask.astype(BF16), before, preferred_element_type=F32)
    return ranks.astype(jnp.int32)


def shards(out_grad, count, chosen, gates, x_slots, w_in, w_out):
    tok_rows, width = out_grad.shape[1:]
    experts, cap = chosen.shape[1:]
    slots = experts * cap
    owners = lax.axis_size("expert")
    per_peer = 3 * tok_rows // owners
    places = owners * per_peer
    me = lax.axis_index("expert")

    x_own = x_slots[0]
    w_in_other = swap(w_in, 1)
    x_other = swap(x_own, 2)
    w_out_other = swap(w_out, 1)

    tokens = chosen.reshape(slots)
    table = lax.all_gather(jnp.concatenate([tokens, count[0]]), "expert", axis=0)
    all_tokens, all_counts = table[:, :slots], table[:, slots:].reshape(-1)

    asked = all_tokens // tok_rows == me
    rank = running_rank(asked)
    local = all_tokens % tok_rows
    place = jnp.where(asked, rank, per_peer)
    picks = place[:, None, :] == jnp.arange(per_peer)[None, :, None]
    row_of = jnp.sum(jnp.where(picks, local[:, None, :] + 1, 0), axis=2).reshape(places) - 1
    send_pick = (row_of[:, None] == jnp.arange(tok_rows)[None, :]).astype(BF16)
    sent = jnp.dot(send_pick, out_grad[0], preferred_element_type=F32).astype(BF16)
    got = lax.all_to_all(
        sent.reshape(owners, per_peer, width), "expert", split_axis=0, concat_axis=0, tiled=True
    ).reshape(places, width)

    source = tokens // tok_rows
    from_source = source[None, :] == jnp.arange(owners)[:, None]
    slot_rank = jnp.sum(jnp.where(from_source, running_rank(from_source), 0), axis=0)
    slot_place = source * per_peer + slot_rank
    slot_pick = (slot_place[:, None] == jnp.arange(places)[None, :]).astype(BF16)
    slot_grad = jnp.dot(slot_pick, got, preferred_element_type=F32).astype(BF16)
    slot_count = jnp.sum(
        jnp.where(tokens[:, None] == jnp.arange(owners * tok_rows)[None, :], all_counts[None, :], 0),
        axis=1,
    ).astype(F32)
    slot_scale = gates.reshape(slots) / slot_count
    own_scalars = jnp.stack([slot_scale, slot_count]).reshape(2, experts, cap)
    grad_own = slot_grad.reshape(experts, cap, width)
    other_scalars = swap(own_scalars, 2)
    grad_other = swap(grad_own, 2)

    inputs = jnp.concatenate([x_own, x_other], axis=1)
    proj_in = jnp.concatenate([w_in, w_in_other], axis=2)
    proj_out = jnp.concatenate([w_out, w_out_other], axis=1)
    upstream = jnp.concatenate([grad_own, grad_other], axis=1)
    scale, counts = jnp.concatenate([own_scalars, other_scalars], axis=2)

    pre = jnp.einsum("ecd,edf->ecf", inputs, proj_in, preferred_element_type=F32)
    normal_cdf = 0.5 * (1.0 + lax.erf(pre * SQRT_HALF))
    slope = normal_cdf + pre * jnp.exp(-0.5 * pre * pre) * INV_ROOT_TWO_PI
    hidden = (pre * normal_cdf).astype(BF16)

    out_slot = (scale[..., None] * upstream.astype(F32)).astype(BF16)
    quarter = w_in.shape[2]
    grad_out_other = jnp.einsum(
        "ecf,ecd->efd", hidden[..., quarter:], out_slot, preferred_element_type=F32
    ).astype(BF16)
    grad_out_got = swap(grad_out_other, 1)

    project = jnp.einsum("ecd,efd->ecf", upstream, proj_out, preferred_element_type=F32)
    gate_part = jnp.sum(hidden.astype(F32) * project, axis=2) / counts
    pre_grad = (scale[..., None] * project * slope).astype(BF16)
    back_other = jnp.einsum(
        "ecf,edf->ecd", pre_grad[:, cap:], proj_in, preferred_element_type=F32
    ).astype(BF16)
    back_got = swap(back_other, 2)
    gate_got = swap(gate_part[:, cap:], 2)
    grad_in_other = jnp.einsum(
        "ecd,ecf->edf", inputs, pre_grad[..., quarter:], preferred_element_type=F32
    ).astype(BF16)
    grad_in_got = swap(grad_in_other, 1)

    back_own = jnp.einsum("ecf,edf->ecd", pre_grad[:, :cap], proj_in, preferred_element_type=F32)
    slot_back = (back_own + back_got.astype(F32)).astype(BF16).reshape(slots, width)
    outgoing = jnp.dot(slot_pick.T, slot_back, preferred_element_type=F32).astype(BF16)
    returned = lax.all_to_all(
        outgoing.reshape(owners, per_peer, width), "expert", split_axis=0, concat_axis=0, tiled=True
    ).reshape(places, width)

    grad_out_own = jnp.einsum(
        "ecf,ecd->efd", hidden[..., :quarter], out_slot, preferred_element_type=F32
    )
    w_out_grad = (grad_out_own + grad_out_got.astype(F32)).astype(BF16)
    grad_in_own = jnp.einsum(
        "ecd,ecf->edf", inputs, pre_grad[..., :quarter], preferred_element_type=F32
    )
    w_in_grad = (grad_in_own + grad_in_got.astype(F32)).astype(BF16)
    token_grad = jnp.dot(send_pick.T, returned, preferred_element_type=F32).astype(BF16)
    gate_grad = gate_part[:, :cap] + gate_got
    return token_grad[None], gate_grad[None], w_in_grad, w_out_grad


def solution(mesh):
    return jax.shard_map(
        shards,
        mesh=mesh,
        in_specs=(
            P("dp", "expert", None),
            P("dp", "expert"),
            P("dp", "expert", None),
            P("dp", "expert", None),
            P("dp", "expert", None, None),
            P("expert", None, "dp"),
            P("expert", "dp", None),
        ),
        out_specs=(
            P("dp", "expert", None),
            P("dp", "expert", None),
            P("expert", None, "dp"),
            P("expert", "dp", None),
        ),
        check_vma=False,
    )
```

time: 487 us -> 316 us (0.65); the launches traced: 480 us -> 315 us
  waiting for transfers between devices: 314 us -> 237 us
  other arithmetic: 41.1 us -> 1.92 us
  local copies, waits for them, and re-layouts: 28.5 us -> 3.09 us
  blocking collectives: 37 us -> 14.4 us
  between operations: 15 us -> 0.91 us
  starting transfers between devices: 9.57 us -> 20.2 us
    ppermute x0 -> x9, waiting for transfers between devices: none -> 172 us  [swap(): return lax.ppermute(value, 'dp', [(i, i ^ bit) for i in range(size)])]
    reduce_scatter x1 -> x0, waiting for transfers between devices: 154 us -> none  [shards(): lax.psum_scatter(back_part.reshape(groups * slots, width), 'dp', scatter_...]
    all_gather x2 -> x0, waiting for transfers between devices: 61.2 us -> none  [the longest x1 61.2 us: shards(): lax.all_gather(slot_grad, 'dp', axis=0, tiled=True)]
    all_to_all x1, waiting for transfers between devices: 26.8 us -> 0.01 us  [shards(): lax.all_to_all(outgoing.reshape(owners, per_peer, width), 'expert', split...]
    all_to_all x2 -> x0, blocking collectives: 19.6 us -> none  [the longest x1 11.7 us: shards(): lax.all_to_all(request.reshape(owners, per_peer), 'expert', split_axis=0,...]
    gather x5 -> x0, local copies, waits for them, and re-layouts: 16.3 us -> none  [the longest x1 7.51 us: shards(): slot_grad = got_rows.reshape(owners * per_peer, width)[slot_place]]
    scatter-add x1 -> x0, other arithmetic: 11.8 us -> none  [shards(): token_sum = jnp.zeros((tok_rows, width), jnp.float32).at[target].add(retu...]
    reduce_sum x3 -> x2, other arithmetic: 12.1 us -> 0.5 us  [the longest x1 0.28 us: shards(): jnp.sum(jnp.where(tokens[:, None] == jnp.arange(owners * tok_rows)[None,...]
  transfers between devices with their start and end apart: 5 -> 11, of which waited for: 4 -> 6; matrix products, arithmetic and copies ran while one was open for 14% -> 7% of each run, Pallas kernels for 0% -> 0%
where the time goes in v1:
time: 316 us; the launch traced here: 315 us
  waiting for transfers between devices  237 us (75%)
  matrix products  37.9 us (12%)
  starting transfers between devices  20.2 us (6%)
  blocking collectives  14.4 us (5%)
    ppermute x9, waiting for transfers between devices, swap(): return lax.ppermute(value, 'dp', [(i, i ^ bit) for i in range(size)])  172 us
    all_to_all x1, waiting for transfers between devices, shards(): lax.all_to_all(sent.reshape(owners, per_peer, width), 'expert', split_axi...  64.8 us
    all_gather x1, blocking collectives, shards(): lax.all_gather(jnp.concatenate([tokens, count[0]]), 'expert', axis=0)  14.4 us
    ppermute x9, starting transfers between devices, swap(): return lax.ppermute(value, 'dp', [(i, i ^ bit) for i in range(size)])  11 us
  transfers between devices with their start and end apart: 11, of which 6 were waited for; matrix products, arithmetic and copies ran while one was open for 7% of the time, Pallas kernels for 0%

profile of v1, /device:TPU:0, one launch (start us, length us, event | category | flops | bytes accessed | tf_op | source)
XLA Modules:
  0.0 315.1 jit_solution(1814304727433098083)
XLA Ops:
  0.6 0.8 pad_add_fusion
  1.4 14.4 %all-gather.1 = s32[8,1,384]{2,1,0:T(1,128)S(1)} all-gather(s32[1,1,384]{2,1,0:T(1,128)S(1)} %reshape.130), channel_id=2, replica_groups=mesh['dp'=4,'expert'=8] {'expert'}, dimensions={0}, use_global_device_ids=true | all-gather | bytes 13824 | tf_op jit(solution)/shard_map/all_gather | solution.py:39
  16.3 2.7 convolution_convert_fusion.1
  19.0 4.4 %all-to-all-start = ((bf16[8,48,4096]{2,1,0:T(8,128)(2,1)}), bf16[8,48,4096]{2,1,0:T(8,128)(2,1)}, u32[]{:S(2)}, u32[]{:S(2)}) async-start(bf16[8,48,4096]{2,1,0:T(8,128)(2,1)} %bitcast.39), calls=%async_computation | async-start | bytes 6291456 | tf_op jit(solution)/shard_map/all_to_all | solution.py:50
  23.5 2.9 copy.32
  26.4 1.6 collective-permute-start.4
  28.0 1.5 collective-permute-start.3
  30.2 64.8 %all-to-all-done = bf16[8,48,4096]{2,1,0:T(8,128)(2,1)} async-done(((bf16[8,48,4096]{2,1,0:T(8,128)(2,1)}), bf16[8,48,4096]{2,1,0:T(8,128)(2,1)}, u32[]{:S(2)}, u32[]{:S(2)}) %all-to-all-start) | async-done | bytes 3145760 | tf_op jit(solution)/shard_map/all_to_all | solution.py:50
  95.0 3.3 %convolution_convert_fusion.5 = bf16[256,4096]{1,0:T(8,128)(2,1)S(1)} fusion(bf16[384,4096]{1,0:T(8,128)(2,1)} %bitcast.7, s32[256]{0:T(256)S(1)} %multiply_add_fusion), kind=kOutput, calls=%fused_computation.10 | convolution fusion | flops 806453248 | bytes 5243904 | tf_op jit(solution)/shard_map/dot_general | solution.py:59
  98.3 1.6 collective-permute-start.1
  100.2 0.6 collective-permute-start
  100.8 44.8 %collective-permute-done = f32[2,2,128]{2,1,0:T(2,128)S(1)} collective-permute-done((f32[2,2,128]{2,1,0:T(2,128)S(1)}, f32[2,2,128]{2,1,0:T(2,128)S(1)}, u32[]{:S(2)}, u32[]{:S(2)}) %collective-permute-start) | collective-permute-done | bytes 2080 | tf_op jit(solution)/shard_map/ppermute | solution.py:14
  145.7 3.7 %fusion.8 = f32[2,256,256]{1,2,0:T(8,128)S(1)} fusion(bf16[2,4096,128]{1,2,0:T(8,128)(2,1)} %collective-permute-done.4, bf16[2,4096,128]{1,2,0:T(8,128)(2,1)S(1)} %copy.32, bf16[2,128,4096]{2,1,0:T(8,128)(2,1)} %collective-permute-done.3, bf16[2,128,4096]{2,1,0:T(8,128)(2,1)S(1)} %bitcast.51), kind=kOutput, calls=%fused_computation.22 | convolution fusion | flops 1090519040 | bytes 8912896 | tf_op jit(solution)/shard_map/ecd,edf->ecf/dot_general | solution.py:76
  149.4 4.5 %multiply_reduce_fusion = (f32[2,256]{1,0:T(2,128)S(1)}, bf16[2,256,256]{1,2,0:T(8,128)(2,1)}, bf16[2,256,256]{1,2,0:T(8,128)(2,1)S(1)}) fusion(f32[2,256,256]{1,2,0:T(8,128)S(1)} %fusion.8, f32[2,256]{1,0:T(2,128)S(1)} %slice_bitcast_fusion.2, bf16[2,128,4096]{2,1,0:T(8,128)(2,1)} %collective-permute-done.2, bf16[2,128,4096]{2,1,0:T(8,128)(2,1)S(1)} %copy-done.5, ...), kind=kOutput, calls=%fused_computation.38 | convolution fusion | flops 1092615680 | bytes 9441280 | tf_op jit(solution)/shard_map/ecd,efd->ecf/dot_general | solution.py:88
  153.9 2.4 convolution_convert_fusion.4
  156.2 1.6 collective-permute-start.5
  157.8 44.7 %collective-permute-done.5 = bf16[2,128,4096]{2,1,0:T(8,128)(2,1)S(1)} collective-permute-done((bf16[2,128,4096]{2,1,0:T(8,128)(2,1)S(1)}, bf16[2,128,4096]{2,1,0:T(8,128)(2,1)S(1)}, u32[]{:S(2)}, u32[]{:S(2)}) %collective-permute-start.5) | collective-permute-done | bytes 2097184 | tf_op jit(solution)/shard_map/ppermute | solution.py:14
  202.6 2.4 fusion
  205.0 2.8 convolution_convert_fusion
  207.8 4.8 %all-to-all-start.1 = ((bf16[8,48,4096]{2,1,0:T(8,128)(2,1)}), bf16[8,48,4096]{2,1,0:T(8,128)(2,1)}, u32[]{:S(2)}, u32[]{:S(2)}) async-start(bf16[8,48,4096]{2,1,0:T(8,128)(2,1)} %bitcast.38), calls=%async_computation.1 | async-start | bytes 6291456 | tf_op jit(solution)/shard_map/all_to_all | solution.py:104
  212.6 3.5 %convolution_convert_fusion.3 = bf16[2,4096,128]{2,1,0:T(8,128)(2,1)S(1)} fusion(bf16[2,128,4096]{2,1,0:T(8,128)(2,1)} %collective-permute-done.3, bf16[2,128,4096]{2,1,0:T(8,128)(2,1)S(1)} %bitcast.52, bf16[2,256,256]{1,2,0:T(8,128)(2,1)S(1)} %get-tuple-element.8), kind=kOutput, calls=%fused_computation.8 | convolution fusion | flops 546308096 | bytes 6422528 | tf_op jit(solution)/shard_map/ecd,ecf->edf/dot_general | solution.py:96
  216.1 1.6 collective-permute-start.7
  217.7 1.4 convolution_convert_fusion.2
  219.1 0.6 collective-permute-start.8
  219.7 1.5 collective-permute-start.6
  221.2 2.0 collective-permute-done.6
  223.2 0.6 fusion.41
  223.8 40.8 %collective-permute-done.7 = bf16[2,4096,128]{2,1,0:T(8,128)(2,1)S(1)} collective-permute-done((bf16[2,4096,128]{2,1,0:T(8,128)(2,1)S(1)}, bf16[2,4096,128]{2,1,0:T(8,128)(2,1)S(1)}, u32[]{:S(2)}, u32[]{:S(2)}) %collective-permute-start.7) | collective-permute-done | bytes 2097184 | tf_op jit(solution)/shard_map/ppermute | solution.py:14
  264.7 4.8 %fusion.1 = bf16[2,4096,128]{2,1,0:T(8,128)(2,1)} fusion(bf16[2,4096,128]{2,1,0:T(8,128)(2,1)S(1)} %collective-permute-done.7, bf16[2,128,4096]{2,1,0:T(8,128)(2,1)} %collective-permute-done.3, bf16[2,128,4096]{2,1,0:T(8,128)(2,1)S(1)} %bitcast.53, bf16[2,256,256]{1,2,0:T(8,128)(2,1)S(1)} %get-tuple-element.8), kind=kOutput, calls=%fused_computation.6 | convolution fusion | flops 548405248 | bytes 8519680 | tf_op jit(solution)/shard_map/ecd,ecf->edf/dot_general | solution.py:112
  269.4 39.4 %collective-permute-done.8 = bf16[2,128,4096]{2,1,0:T(8,128)(2,1)S(1)} collective-permute-done((bf16[2,128,4096]{2,1,0:T(8,128)(2,1)S(1)}, bf16[2,128,4096]{2,1,0:T(8,128)(2,1)S(1)}, u32[]{:S(2)}, u32[]{:S(2)}) %collective-permute-start.8) | collective-permute-done | bytes 2097184 | tf_op jit(solution)/shard_map/ppermute | solution.py:14
  308.8 2.5 add_convert_fusion
  311.4 3.7 %fusion.2 = bf16[1,128,4096]{2,1,0:T(8,128)(2,1)} fusion(bf16[384,4096]{1,0:T(8,128)(2,1)} %bitcast.12, s32[384]{0:T(512)S(1)} %sub.20), kind=kOutput, calls=%fused_computation.12 | convolution fusion | flops 403226624 | bytes 4195840 | tf_op jit(solution)/shard_map/dot_general | solution.py:116
  (47 shorter events, 1.6 us)
Async XLA Ops:
  0.6 15.7 %copy-start = (bf16[1,128,4096]{2,1,0:T(8,128)(2,1)S(1)}, bf16[1,128,4096]{2,1,0:T(8,128)(2,1)}, u32[]{:S(2)}) copy-start(bf16[1,128,4096]{2,1,0:T(8,128)(2,1)} %param.7) | copy-start | bytes 3145732
  19.0 76.0 %all-to-all-start = ((bf16[8,48,4096]{2,1,0:T(8,128)(2,1)}), bf16[8,48,4096]{2,1,0:T(8,128)(2,1)}, u32[]{:S(2)}, u32[]{:S(2)}) async-start(bf16[8,48,4096]{2,1,0:T(8,128)(2,1)} %bitcast.39), calls=%async_computation | async-start | bytes 6291456 | tf_op jit(solution)/shard_map/all_to_all | solution.py:50
  23.4 6.6 %copy-start.3 = (s32[1,2,128]{2,1,0:T(2,128)S(1)}, s32[1,2,128]{2,1,0:T(2,128)}, u32[]{:S(2)}) copy-start(s32[1,2,128]{2,1,0:T(2,128)} %param.9) | copy-start | bytes 3076
  26.4 73.8 %copy-start.4 = (f32[1,2,128]{2,1,0:T(2,128)S(1)}, f32[1,2,128]{2,1,0:T(2,128)}, u32[]{:S(2)}) copy-start(f32[1,2,128]{2,1,0:T(2,128)} %param.10) | copy-start | bytes 3076
  26.4 119.2 %collective-permute-start.4 = (bf16[2,4096,128]{1,2,0:T(8,128)(2,1)S(1)}, bf16[2,4096,128]{1,2,0:T(8,128)(2,1)}, u32[]{:S(2)}, u32[]{:S(2)}) collective-permute-start(bf16[2,4096,128]{1,2,0:T(8,128)(2,1)S(1)} %copy.32), channel_id=1, source_target_pairs={{0,8},{8,0},{16,24},{24,16},{1,9},{9,1},{17,25},{25,17},{2,10},{10... | collective-permute-start | bytes 6291464 | tf_op jit(solution)/shard_map/ppermute | solution.py:14
  28.0 117.7 %collective-permute-start.3 = (bf16[2,128,4096]{2,1,0:T(8,128)(2,1)}, bf16[2,128,4096]{2,1,0:T(8,128)(2,1)}, u32[]{:S(2)}, u32[]{:S(2)}) collective-permute-start(bf16[2,128,4096]{2,1,0:T(8,128)(2,1)} %bitcast.50), channel_id=1, source_target_pairs={{0,16},{8,24},{16,0},{24,8},{1,17},{9,25},{17,1},{25,9},{2,18},{10... | collective-permute-start | bytes 6291464 | tf_op jit(solution)/shard_map/ppermute | solution.py:14
  29.5 119.8 %collective-permute-start.2 = (bf16[2,128,4096]{2,1,0:T(8,128)(2,1)}, bf16[2,128,4096]{2,1,0:T(8,128)(2,1)}, u32[]{:S(2)}, u32[]{:S(2)}) collective-permute-start(bf16[2,128,4096]{2,1,0:T(8,128)(2,1)} %param.13), channel_id=1, source_target_pairs={{0,8},{8,0},{16,24},{24,16},{1,9},{9,1},{17,25},{25,17},{2,10},{10... | collective-permute-start | bytes 6291464 | tf_op jit(solution)/shard_map/ppermute | solution.py:14
  95.0 50.7 %copy-start.6 = (bf16[1,2,128,4096]{3,2,1,0:T(8,128)(2,1)S(1)}, bf16[1,2,128,4096]{3,2,1,0:T(8,128)(2,1)}, u32[]{:S(2)}) copy-start(bf16[1,2,128,4096]{3,2,1,0:T(8,128)(2,1)} %param.11) | copy-start | bytes 6291460
  98.3 51.0 %copy-start.1 = (bf16[256,4096]{1,0:T(8,128)(2,1)}, bf16[256,4096]{1,0:T(8,128)(2,1)S(1)}, u32[]{:S(2)}) copy-start(bf16[256,4096]{1,0:T(8,128)(2,1)S(1)} %convolution_convert_fusion.5) | copy-start | bytes 6291460
  98.3 51.0 %collective-permute-start.1 = (bf16[2,128,4096]{2,1,0:T(8,128)(2,1)S(1)}, bf16[2,128,4096]{2,1,0:T(8,128)(2,1)S(1)}, u32[]{:S(2)}, u32[]{:S(2)}) collective-permute-start(bf16[2,128,4096]{2,1,0:T(8,128)(2,1)S(1)} %bitcast.40), channel_id=1, source_target_pairs={{0,16},{8,24},{16,0},{24,8},{1,17},{9,25},{17,1},{25,9},{2,18},{10... | collective-permute-start | bytes 6291464 | tf_op jit(solution)/shard_map/ppermute | solution.py:14
  100.2 45.4 %collective-permute-start = (f32[2,2,128]{2,1,0:T(2,128)S(1)}, f32[2,2,128]{2,1,0:T(2,128)S(1)}, u32[]{:S(2)}, u32[]{:S(2)}) collective-permute-start(f32[2,2,128]{2,1,0:T(2,128)S(1)} %pad_maximum_fusion.13), channel_id=1, source_target_pairs={{0,16},{8,24},{16,0},{24,8},{1,17},{9,25},{17,1},{25,9},{2,18},{10... | collective-permute-start | bytes 6152 | tf_op jit(solution)/shard_map/ppermute | solution.py:14
  145.6 3.7 %copy-start.5 = (bf16[2,128,4096]{2,1,0:T(8,128)(2,1)S(1)}, bf16[2,128,4096]{2,1,0:T(8,128)(2,1)}, u32[]{:S(2)}) copy-start(bf16[2,128,4096]{2,1,0:T(8,128)(2,1)} %param.13) | copy-start | bytes 6291460
  149.4 4.5 %copy-start.8 = (bf16[2,128,4096]{2,1,0:T(8,128)(2,1)}, bf16[2,128,4096]{2,1,0:T(8,128)(2,1)S(1)}, u32[]{:S(2)}) copy-start(bf16[2,128,4096]{2,1,0:T(8,128)(2,1)S(1)} %collective-permute-done.1) | copy-start | bytes 6291460
  156.2 46.3 %collective-permute-start.5 = (bf16[2,128,4096]{2,1,0:T(8,128)(2,1)S(1)}, bf16[2,128,4096]{2,1,0:T(8,128)(2,1)S(1)}, u32[]{:S(2)}, u32[]{:S(2)}) collective-permute-start(bf16[2,128,4096]{2,1,0:T(8,128)(2,1)S(1)} %convolution_convert_fusion.4), channel_id=1, source_target_pairs={{0,16},{8,24},{16,0},{24,8},{1,17},{9,25},{17,1},{25,9},{2,18},{10... | collective-permute-start | bytes 6291464 | tf_op jit(solution)/shard_map/ppermute | solution.py:14
  207.8 4.8 %copy-start.7 = (bf16[1,2,128,4096]{3,2,1,0:T(8,128)(2,1)S(1)}, bf16[1,2,128,4096]{3,2,1,0:T(8,128)(2,1)}, u32[]{:S(2)}) copy-start(bf16[1,2,128,4096]{3,2,1,0:T(8,128)(2,1)} %param.11) | copy-start | bytes 6291460
  207.8 103.6 %all-to-all-start.1 = ((bf16[8,48,4096]{2,1,0:T(8,128)(2,1)}), bf16[8,48,4096]{2,1,0:T(8,128)(2,1)}, u32[]{:S(2)}, u32[]{:S(2)}) async-start(bf16[8,48,4096]{2,1,0:T(8,128)(2,1)} %bitcast.38), calls=%async_computation.1 | async-start | bytes 6291456 | tf_op jit(solution)/shard_map/all_to_all | solution.py:104
  212.5 5.1 %copy-start.2 = (bf16[256,4096]{1,0:T(8,128)(2,1)S(1)}, bf16[256,4096]{1,0:T(8,128)(2,1)}, u32[]{:S(2)}) copy-start(bf16[256,4096]{1,0:T(8,128)(2,1)} %copy-done.1) | copy-start | bytes 6291460
  212.6 5.1 %copy-start.9 = (bf16[2,128,4096]{2,1,0:T(8,128)(2,1)S(1)}, bf16[2,128,4096]{2,1,0:T(8,128)(2,1)}, u32[]{:S(2)}) copy-start(bf16[2,128,4096]{2,1,0:T(8,128)(2,1)} %copy-done.8) | copy-start | bytes 6291460
  212.6 5.1 %copy-start.10 = (bf16[2,256,256]{1,2,0:T(8,128)(2,1)S(1)}, bf16[2,256,256]{1,2,0:T(8,128)(2,1)}, u32[]{:S(2)}) copy-start(bf16[2,256,256]{1,2,0:T(8,128)(2,1)} %get-tuple-element.5) | copy-start | bytes 786436
  216.1 48.5 %collective-permute-start.7 = (bf16[2,4096,128]{2,1,0:T(8,128)(2,1)S(1)}, bf16[2,4096,128]{2,1,0:T(8,128)(2,1)S(1)}, u32[]{:S(2)}, u32[]{:S(2)}) collective-permute-start(bf16[2,4096,128]{2,1,0:T(8,128)(2,1)S(1)} %convolution_convert_fusion.3), channel_id=1, source_target_pairs={{0,8},{8,0},{16,24},{24,16},{1,9},{9,1},{17,25},{25,17},{2,10},{10... | collective-permute-start | bytes 6291464 | tf_op jit(solution)/shard_map/ppermute | solution.py:14
  219.1 89.8 %collective-permute-start.8 = (bf16[2,128,4096]{2,1,0:T(8,128)(2,1)S(1)}, bf16[2,128,4096]{2,1,0:T(8,128)(2,1)S(1)}, u32[]{:S(2)}, u32[]{:S(2)}) collective-permute-start(bf16[2,128,4096]{2,1,0:T(8,128)(2,1)S(1)} %convolution_convert_fusion.2), channel_id=1, source_target_pairs={{0,8},{8,0},{16,24},{24,16},{1,9},{9,1},{17,25},{25,17},{2,10},{10... | collective-permute-start | bytes 6291464 | tf_op jit(solution)/shard_map/ppermute | solution.py:14
  219.7 3.6 %collective-permute-start.6 = (f32[2,128]{1,0:T(2,128)S(1)}, f32[2,128]{1,0:T(2,128)S(1)}, u32[]{:S(2)}, u32[]{:S(2)}) collective-permute-start(f32[2,128]{1,0:T(2,128)S(1)} %slice.45), channel_id=1, source_target_pairs={{0,16},{8,24},{16,0},{24,8},{1,17},{9,25},{17,1},{25,9},{2,18},{10... | collective-permute-start | bytes 3080 | tf_op jit(solution)/shard_map/ppermute | solution.py:14

commit v2 on v1

v2 whole, which is shorter than its diff:
```python
import jax
import jax.numpy as jnp
from jax import lax
from jax.sharding import PartitionSpec as P

SQRT_HALF = 0.7071067811865476
INV_ROOT_TWO_PI = 0.3989422804014327
BF16 = jnp.bfloat16
F32 = jnp.float32
PARTS = 2


def swap(value, bit):
    size = lax.axis_size("dp")
    return lax.ppermute(value, "dp", [(i, i ^ bit) for i in range(size)])


def exchange(rows, owners):
    blocks = rows.reshape(owners, -1, rows.shape[1])
    got = lax.all_to_all(blocks, "expert", split_axis=0, concat_axis=0, tiled=True)
    return got.reshape(rows.shape)


def running_rank(mask):
    n = mask.shape[-1]
    before = (jnp.arange(n)[:, None] < jnp.arange(n)[None, :]).astype(BF16)
    ranks = jnp.dot(mask.astype(BF16), before, preferred_element_type=F32)
    return ranks.astype(jnp.int32)


def shards(out_grad, count, chosen, gates, x_slots, w_in, w_out):
    tok_rows, width = out_grad.shape[1:]
    experts, cap = chosen.shape[1:]
    slots = experts * cap
    owners = lax.axis_size("expert")
    per_peer = 3 * tok_rows // owners
    places = owners * per_peer
    me = lax.axis_index("expert")

    x_own = x_slots[0]
    w_in_other = swap(w_in, 1)
    x_other = swap(x_own, 2)
    w_out_other = swap(w_out, 1)

    tokens = chosen.reshape(slots)
    table = lax.all_gather(jnp.concatenate([tokens, count[0]]), "expert", axis=0)
    all_tokens, all_counts = table[:, :slots], table[:, slots:].reshape(-1)

    asked = all_tokens // tok_rows == me
    rank = running_rank(asked)
    local = all_tokens % tok_rows
    place = jnp.where(asked, rank, per_peer)
    picks = place[:, None, :] == jnp.arange(per_peer)[None, :, None]
    row_of = jnp.sum(jnp.where(picks, local[:, None, :] + 1, 0), axis=2).reshape(places) - 1
    send_pick = (row_of[:, None] == jnp.arange(tok_rows)[None, :]).astype(BF16)

    source = tokens // tok_rows
    from_source = source[None, :] == jnp.arange(owners)[:, None]
    slot_rank = jnp.sum(jnp.where(from_source, running_rank(from_source), 0), axis=0)
    slot_place = source * per_peer + slot_rank
    slot_pick = (slot_place[:, None] == jnp.arange(places)[None, :]).astype(BF16)
    slot_count = jnp.sum(
        jnp.where(tokens[:, None] == jnp.arange(owners * tok_rows)[None, :], all_counts[None, :], 0),
        axis=1,
    ).astype(F32)
    slot_scale = gates.reshape(slots) / slot_count
    own_scalars = jnp.stack([slot_scale, slot_count]).reshape(2, experts, cap)
    other_scalars = swap(own_scalars, 2)

    part = width // PARTS
    columns = [slice(k * part, (k + 1) * part) for k in range(PARTS)]
    upstream = []
    for cols in columns:
        sent = jnp.dot(send_pick, out_grad[0][:, cols], preferred_element_type=F32).astype(BF16)
        got = exchange(sent, owners)
        grad_own = jnp.dot(slot_pick, got, preferred_element_type=F32).astype(BF16)
        grad_own = grad_own.reshape(experts, cap, part)
        upstream.append(jnp.concatenate([grad_own, swap(grad_own, 2)], axis=1))

    inputs = jnp.concatenate([x_own, x_other], axis=1)
    proj_in = jnp.concatenate([w_in, w_in_other], axis=2)
    proj_out = jnp.concatenate([w_out, w_out_other], axis=1)
    scale, counts = jnp.concatenate([own_scalars, other_scalars], axis=2)

    pre = jnp.einsum("ecd,edf->ecf", inputs, proj_in, preferred_element_type=F32)
    normal_cdf = 0.5 * (1.0 + lax.erf(pre * SQRT_HALF))
    slope = normal_cdf + pre * jnp.exp(-0.5 * pre * pre) * INV_ROOT_TWO_PI
    hidden = (pre * normal_cdf).astype(BF16)

    out_slot = [(scale[..., None] * u.astype(F32)).astype(BF16) for u in upstream]
    quarter = w_in.shape[2]
    project = sum(
        jnp.einsum("ecd,efd->ecf", u, proj_out[..., cols], preferred_element_type=F32)
        for u, cols in zip(upstream, columns)
    )
    gate_part = jnp.sum(hidden.astype(F32) * project, axis=2) / counts
    pre_grad = (scale[..., None] * project * slope).astype(BF16)
    gate_got = swap(gate_part[:, cap:], 2)

    def grad_out(units):
        terms = [jnp.einsum("ecf,ecd->efd", units, o, preferred_element_type=F32) for o in out_slot]
        return jnp.concatenate(terms, axis=2)

    def grad_in(units):
        return jnp.einsum("ecd,ecf->edf", inputs, units, preferred_element_type=F32)

    back_got = []
    for k, cols in enumerate(columns):
        back_other = jnp.einsum(
            "ecf,edf->ecd", pre_grad[:, cap:], proj_in[:, cols], preferred_element_type=F32
        ).astype(BF16)
        if k == 0:
            grad_out_other = grad_out(hidden[..., quarter:]).astype(BF16)
            back_other, grad_out_other = lax.optimization_barrier((back_other, grad_out_other))
            grad_out_got = swap(grad_out_other, 1)
        if k == PARTS - 1:
            grad_in_other = grad_in(pre_grad[..., quarter:]).astype(BF16)
            back_other, grad_in_other = lax.optimization_barrier((back_other, grad_in_other))
            grad_in_got = swap(grad_in_other, 1)
        back_got.append(swap(back_other, 2))

    returned = []
    for k, cols in enumerate(columns):
        back_own = jnp.einsum(
            "ecf,edf->ecd", pre_grad[:, :cap], proj_in[:, cols], preferred_element_type=F32
        )
        slot_back = (back_own + back_got[k].astype(F32)).astype(BF16).reshape(slots, part)
        outgoing = jnp.dot(slot_pick.T, slot_back, preferred_element_type=F32).astype(BF16)
        if k == PARTS - 1:
            outgoing, grad_out_got = lax.optimization_barrier((outgoing, grad_out_got))
        returned.append(exchange(outgoing, owners))

    w_out_grad = (grad_out(hidden[..., :quarter]) + grad_out_got.astype(F32)).astype(BF16)
    returned[-1], grad_in_got = lax.optimization_barrier((returned[-1], grad_in_got))
    w_in_grad = (grad_in(pre_grad[..., :quarter]) + grad_in_got.astype(F32)).astype(BF16)
    token_grad = jnp.concatenate(
        [jnp.dot(send_pick.T, r, preferred_element_type=F32).astype(BF16) for r in returned], axis=1
    )
    gate_grad = gate_part[:, :cap] + gate_got
    return token_grad[None], gate_grad[None], w_in_grad, w_out_grad


def solution(mesh):
    return jax.shard_map(
        shards,
        mesh=mesh,
        in_specs=(
            P("dp", "expert", None),
            P("dp", "expert"),
            P("dp", "expert", None),
            P("dp", "expert", None),
            P("dp", "expert", None, None),
            P("expert", None, "dp"),
            P("expert", "dp", None),
        ),
        out_specs=(
            P("dp", "expert", None),
            P("dp", "expert", None),
            P("expert", None, "dp"),
            P("expert", "dp", None),
        ),
        check_vma=False,
    )
```

time: 316 us -> 315 us (level)
  waiting for transfers between devices: 237 us -> 206 us
  starting transfers between devices: 20.2 us -> 30.6 us
  matrix products: 37.9 us -> 44.4 us
  local copies, waits for them, and re-layouts: 3.09 us -> 9.19 us
  other arithmetic: 1.92 us -> 7.96 us
    all_to_all x2 -> x4, waiting for transfers between devices: 64.8 us -> 36 us  [exchange(): lax.all_to_all(blocks, 'expert', split_axis=0, concat_axis=0, tiled=True)]
    all_to_all x2 -> x4, starting transfers between devices: 9.19 us -> 16.6 us  [exchange(): lax.all_to_all(blocks, 'expert', split_axis=0, concat_axis=0, tiled=True)]
    dot_general x10 -> x18, matrix products: 31.2 us -> 36.2 us  [the longest x2 10.1 us: grad_in(): return jnp.einsum('ecd,ecf->edf', inputs, units, preferred_element_type=F32)]
    unnamed x25 -> x34, local copies, waits for them, and re-layouts: 3 us -> 7.37 us
    convert_element_type x0 -> x1, other arithmetic: none -> 3.56 us  [shards(): (grad_out(hidden[..., :quarter]) + grad_out_got.astype(F32)).astype(BF16)]
    ppermute x9 -> x11, starting transfers between devices: 11 us -> 14 us  [swap(): return lax.ppermute(value, 'dp', [(i, i ^ bit) for i in range(size)])]
    ppermute x9 -> x11, waiting for transfers between devices: 172 us -> 170 us  [swap(): return lax.ppermute(value, 'dp', [(i, i ^ bit) for i in range(size)])]
  transfers between devices with their start and end apart: 11 -> 15, of which waited for: 6 -> 8; matrix products, arithmetic and copies ran while one was open for 7% -> 13% of each run, Pallas kernels for 0% -> 0%
where the time goes in v2:
time: 315 us; the launch traced here: 314 us
  waiting for transfers between devices  206 us (65%)
  matrix products  44.4 us (14%)
  starting transfers between devices  30.6 us (10%)
  blocking collectives  14.4 us (5%)
  local copies, waits for them, and re-layouts  9.19 us (3%)
  other arithmetic  7.96 us (3%)
    ppermute x11, waiting for transfers between devices, swap(): return lax.ppermute(value, 'dp', [(i, i ^ bit) for i in range(size)])  170 us
    all_to_all x4, waiting for transfers between devices, exchange(): lax.all_to_all(blocks, 'expert', split_axis=0, concat_axis=0, tiled=True)  36 us
    all_to_all x4, starting transfers between devices, exchange(): lax.all_to_all(blocks, 'expert', split_axis=0, concat_axis=0, tiled=True)  16.6 us
    all_gather x1, blocking collectives, shards(): lax.all_gather(jnp.concatenate([tokens, count[0]]), 'expert', axis=0)  14.4 us
    ppermute x11, starting transfers between devices, swap(): return lax.ppermute(value, 'dp', [(i, i ^ bit) for i in range(size)])  14 us
    dot_general x2, matrix products, grad_in(): return jnp.einsum('ecd,ecf->edf', inputs, units, preferred_element_type=F32)  10.1 us
    unnamed x34, local copies, waits for them, and re-layouts  7.37 us
    dot_general x4, matrix products, grad_out(): jnp.einsum('ecf,ecd->efd', units, o, preferred_element_type=F32)  6.62 us
  transfers between devices with their start and end apart: 15, of which 8 were waited for; matrix products, arithmetic and copies ran while one was open for 13% of the time, Pallas kernels for 0%

profile of v2, /device:TPU:0, one launch (start us, length us, event | category | flops | bytes accessed | tf_op | source)
XLA Modules:
  0.0 313.7 jit_solution(7163487088298153784)
XLA Ops:
  1.3 14.4 %all-gather.1 = s32[8,1,384]{2,1,0:T(1,128)S(1)} all-gather(s32[1,1,384]{2,1,0:T(1,128)S(1)} %reshape.154), channel_id=2, replica_groups=mesh['dp'=4,'expert'=8] {'expert'}, dimensions={0}, use_global_device_ids=true | all-gather | bytes 13824 | tf_op jit(solution)/shard_map/all_gather | solution.py:46
  16.2 2.8 convolution_convert_fusion.3
  19.0 3.7 %all-to-all-start.1 = ((bf16[8,48,2048]{2,1,0:T(8,128)(2,1)}), bf16[8,48,2048]{2,1,0:T(8,128)(2,1)S(1)}, u32[]{:S(2)}, u32[]{:S(2)}) async-start(bf16[8,48,2048]{2,1,0:T(8,128)(2,1)} %bitcast.9), calls=%async_computation.1 | async-start | bytes 3145728 | tf_op jit(solution)/shard_map/all_to_all | solution.py:20
  22.7 1.8 convolution_convert_fusion.4
  24.5 36.0 %all-to-all-done.1 = bf16[8,48,2048]{2,1,0:T(8,128)(2,1)S(1)} async-done(((bf16[8,48,2048]{2,1,0:T(8,128)(2,1)}), bf16[8,48,2048]{2,1,0:T(8,128)(2,1)S(1)}, u32[]{:S(2)}, u32[]{:S(2)}) %all-to-all-start.1) | async-done | bytes 1572896 | tf_op jit(solution)/shard_map/all_to_all | solution.py:20
  60.5 3.6 %all-to-all-start = ((bf16[8,48,2048]{2,1,0:T(8,128)(2,1)}), bf16[8,48,2048]{2,1,0:T(8,128)(2,1)S(1)}, u32[]{:S(2)}, u32[]{:S(2)}) async-start(bf16[8,48,2048]{2,1,0:T(8,128)(2,1)} %bitcast.6), calls=%async_computation | async-start | bytes 3145728 | tf_op jit(solution)/shard_map/all_to_all | solution.py:20
  65.6 4.1 %copy.40 = bf16[2,4096,128]{1,2,0:T(8,128)(2,1)} copy(bf16[2,4096,128]{2,1,0:T(8,128)(2,1)} %param.12) | data formatting | bytes 4194304 | tf_op args[5]
  72.9 3.1 %constant_dynamic-update-slice_fusion.1 = bf16[2,256,4096]{2,1,0:T(8,128)(2,1)} fusion(bf16[2,128,4096]{2,1,0:T(8,128)(2,1)} %param.13), kind=kLoop, calls=%fused_computation.99 | loop fusion | bytes 4194304
  76.0 41.9 %collective-permute-done = f32[2,2,128]{2,1,0:T(2,128)S(1)} collective-permute-done((f32[2,2,128]{2,1,0:T(2,128)S(1)}, f32[2,2,128]{2,1,0:T(2,128)S(1)}, u32[]{:S(2)}, u32[]{:S(2)}) %collective-permute-start) | collective-permute-done | bytes 2080 | tf_op jit(solution)/shard_map/ppermute | solution.py:15
  117.9 1.7 convolution_convert_fusion.9
  122.5 34.8 %collective-permute-done.5 = bf16[2,4096,128]{1,2,0:T(8,128)(2,1)} collective-permute-done((bf16[2,4096,128]{1,2,0:T(8,128)(2,1)}, bf16[2,4096,128]{1,2,0:T(8,128)(2,1)}, u32[]{:S(2)}, u32[]{:S(2)}) %collective-permute-start.5) | collective-permute-done | bytes 2097184 | tf_op jit(solution)/shard_map/ppermute | solution.py:15
  157.3 4.1 %fusion.1 = f32[2,256,256]{1,2,0:T(8,128)S(1)} fusion(bf16[2,4096,128]{1,2,0:T(8,128)(2,1)} %collective-permute-done.5, bf16[2,4096,128]{1,2,0:T(8,128)(2,1)S(1)} %copy-done, bf16[2,128,4096]{2,1,0:T(8,128)(2,1)} %collective-permute-done.4, bf16[2,128,4096]{2,1,0:T(8,128)(2,1)} %bitcast.63), kind=kOutput, calls=%fused_computation.8 | convolution fusion | flops 1090519040 | bytes 8912896 | tf_op jit(solution)/shard_map/ecd,edf->ecf/dot_general | solution.py:85
  161.4 1.7 constant_dynamic-update-slice_fusion
  163.2 2.3 fusion.7
  167.2 2.0 convolution_convert_fusion.6
  171.4 1.7 convolution_convert_fusion.8
  174.7 22.4 %collective-permute-done.6 = bf16[2,128,2048]{2,1,0:T(8,128)(2,1)S(1)} collective-permute-done((bf16[2,128,2048]{2,1,0:T(8,128)(2,1)S(1)}, bf16[2,128,2048]{2,1,0:T(8,128)(2,1)S(1)}, u32[]{:S(2)}, u32[]{:S(2)}) %collective-permute-start.6) | collective-permute-done | bytes 1048608 | tf_op jit(solution)/shard_map/ppermute | solution.py:15
  197.1 1.7 fusion.3
  198.8 1.9 convolution_convert_fusion.2
  200.7 4.6 %all-to-all-start.2 = ((bf16[8,48,2048]{2,1,0:T(8,128)(2,1)}), bf16[8,48,2048]{2,1,0:T(8,128)(2,1)S(1)}, u32[]{:S(2)}, u32[]{:S(2)}) async-start(bf16[8,48,2048]{2,1,0:T(8,128)(2,1)} %bitcast.14), calls=%async_computation.2 | async-start | bytes 3145728 | tf_op jit(solution)/shard_map/all_to_all | solution.py:20
  206.8 2.0 convolution_convert_fusion.5
  208.9 4.8 %convolution_convert_fusion = bf16[2,4096,128]{2,1,0:T(8,128)(2,1)} fusion(bf16[2,128,4096]{2,1,0:T(8,128)(2,1)} %collective-permute-done.4, bf16[2,128,4096]{2,1,0:T(8,128)(2,1)S(1)} %bitcast.64, bf16[2,256,256]{1,2,0:T(8,128)(2,1)S(1)} %get-tuple-element.24), kind=kOutput, calls=%fused_computation.7 | convolution fusion | flops 546308096 | bytes 6422528 | tf_op jit(solution)/shard_map/ecd,ecf->edf/dot_general | solution.py:105
  215.2 23.7 %collective-permute-done.7 = bf16[2,128,2048]{2,1,0:T(8,128)(2,1)S(1)} collective-permute-done((bf16[2,128,2048]{2,1,0:T(8,128)(2,1)S(1)}, bf16[2,128,2048]{2,1,0:T(8,128)(2,1)S(1)}, u32[]{:S(2)}, u32[]{:S(2)}) %collective-permute-start.7) | collective-permute-done | bytes 1048608 | tf_op jit(solution)/shard_map/ppermute | solution.py:15
  238.9 1.7 fusion.4
  240.7 1.8 convolution_convert_fusion.1
  242.5 11.1 %collective-permute-done.8 = bf16[2,128,4096]{2,1,0:T(8,128)(2,1)} collective-permute-done((bf16[2,128,4096]{2,1,0:T(8,128)(2,1)}, bf16[2,128,4096]{2,1,0:T(8,128)(2,1)}, u32[]{:S(2)}, u32[]{:S(2)}) %collective-permute-start.8) | collective-permute-done | bytes 2097184 | tf_op jit(solution)/shard_map/ppermute | solution.py:15
  253.6 4.7 %all-to-all-start.3 = ((bf16[8,48,2048]{2,1,0:T(8,128)(2,1)}), bf16[8,48,2048]{2,1,0:T(8,128)(2,1)S(1)}, u32[]{:S(2)}, u32[]{:S(2)}) async-start(bf16[8,48,2048]{2,1,0:T(8,128)(2,1)} %bitcast.17), calls=%async_computation.3 | async-start | bytes 3145728 | tf_op jit(solution)/shard_map/all_to_all | solution.py:20
  261.5 2.2 fusion.11
  263.6 1.8 fusion.12
  266.1 3.6 %fusion.2 = bf16[2,128,4096]{2,1,0:T(8,128)(2,1)} fusion(f32[2,128,2048]{2,1,0:T(8,128)S(1)} %fusion.12, f32[2,128,2048]{2,1,0:T(8,128)S(1)} %fusion.11, bf16[2,128,4096]{2,1,0:T(8,128)(2,1)} %collective-permute-done.8), kind=kLoop, calls=%fused_computation.11 | loop fusion | flops 4194304 | bytes 8388608 | tf_op jit(solution)/shard_map/convert_element_type | solution.py:133
  271.0 35.8 %collective-permute-done.9 = bf16[2,4096,128]{2,1,0:T(8,128)(2,1)} collective-permute-done((bf16[2,4096,128]{2,1,0:T(8,128)(2,1)}, bf16[2,4096,128]{2,1,0:T(8,128)(2,1)}, u32[]{:S(2)}, u32[]{:S(2)}) %collective-permute-start.9) | collective-permute-done | bytes 2097184 | tf_op jit(solution)/shard_map/ppermute | solution.py:15
  308.4 5.3 %fusion = bf16[2,4096,128]{2,1,0:T(8,128)(2,1)} fusion(bf16[2,4096,128]{2,1,0:T(8,128)(2,1)} %collective-permute-done.9, bf16[2,128,4096]{2,1,0:T(8,128)(2,1)} %collective-permute-done.4, bf16[2,128,4096]{2,1,0:T(8,128)(2,1)S(1)} %bitcast.65, bf16[2,256,256]{1,2,0:T(8,128)(2,1)S(1)} %copy-done.14), kind=kOutput, calls=%fused_computation.6 | convolution fusion | flops 548405248 | bytes 8519680 | tf_op jit(solution)/shard_map/ecd,ecf->edf/dot_general | solution.py:105
  (77 shorter events, 23.9 us)
Async XLA Ops:
  19.0 3.7 %copy-start.3 = (bf16[1,128,4096]{2,1,0:T(8,128)(2,1)S(1)}, bf16[1,128,4096]{2,1,0:T(8,128)(2,1)}, u32[]{:S(2)}) copy-start(bf16[1,128,4096]{2,1,0:T(8,128)(2,1)} %param.7) | copy-start | bytes 3145732
  19.0 41.5 %all-to-all-start.1 = ((bf16[8,48,2048]{2,1,0:T(8,128)(2,1)}), bf16[8,48,2048]{2,1,0:T(8,128)(2,1)S(1)}, u32[]{:S(2)}, u32[]{:S(2)}) async-start(bf16[8,48,2048]{2,1,0:T(8,128)(2,1)} %bitcast.9), calls=%async_computation.1 | async-start | bytes 3145728 | tf_op jit(solution)/shard_map/all_to_all | solution.py:20
  60.5 60.7 %all-to-all-start = ((bf16[8,48,2048]{2,1,0:T(8,128)(2,1)}), bf16[8,48,2048]{2,1,0:T(8,128)(2,1)S(1)}, u32[]{:S(2)}, u32[]{:S(2)}) async-start(bf16[8,48,2048]{2,1,0:T(8,128)(2,1)} %bitcast.6), calls=%async_computation | async-start | bytes 3145728 | tf_op jit(solution)/shard_map/all_to_all | solution.py:20
  64.1 7.7 %copy-start.6 = (s32[1,2,128]{2,1,0:T(2,128)S(1)}, s32[1,2,128]{2,1,0:T(2,128)}, u32[]{:S(2)}) copy-start(s32[1,2,128]{2,1,0:T(2,128)} %param.9) | copy-start | bytes 3076
  64.1 8.0 %copy-start.7 = (f32[1,2,128]{2,1,0:T(2,128)S(1)}, f32[1,2,128]{2,1,0:T(2,128)}, u32[]{:S(2)}) copy-start(f32[1,2,128]{2,1,0:T(2,128)} %param.10) | copy-start | bytes 3076
  64.1 97.3 %collective-permute-start.2 = (bf16[2,128,4096]{2,1,0:T(8,128)(2,1)}, bf16[2,128,4096]{2,1,0:T(8,128)(2,1)}, u32[]{:S(2)}, u32[]{:S(2)}) collective-permute-start(bf16[2,128,4096]{2,1,0:T(8,128)(2,1)} %param.13), channel_id=1, source_target_pairs={{0,8},{8,0},{16,24},{24,16},{1,9},{9,1},{17,25},{25,17},{2,10},{10... | collective-permute-start | bytes 6291464 | tf_op jit(solution)/shard_map/ppermute | solution.py:15
  69.7 87.5 %collective-permute-start.5 = (bf16[2,4096,128]{1,2,0:T(8,128)(2,1)}, bf16[2,4096,128]{1,2,0:T(8,128)(2,1)}, u32[]{:S(2)}, u32[]{:S(2)}) collective-permute-start(bf16[2,4096,128]{1,2,0:T(8,128)(2,1)} %copy.40), channel_id=1, source_target_pairs={{0,8},{8,0},{16,24},{24,16},{1,9},{9,1},{17,25},{25,17},{2,10},{10... | collective-permute-start | bytes 6291464 | tf_op jit(solution)/shard_map/ppermute | solution.py:15
  70.3 87.0 %collective-permute-start.4 = (bf16[2,128,4096]{2,1,0:T(8,128)(2,1)}, bf16[2,128,4096]{2,1,0:T(8,128)(2,1)}, u32[]{:S(2)}, u32[]{:S(2)}) collective-permute-start(bf16[2,128,4096]{2,1,0:T(8,128)(2,1)} %bitcast.62), channel_id=1, source_target_pairs={{0,16},{8,24},{16,0},{24,8},{1,17},{9,25},{17,1},{25,9},{2,18},{10... | collective-permute-start | bytes 6291464 | tf_op jit(solution)/shard_map/ppermute | solution.py:15
  72.1 45.8 %collective-permute-start = (f32[2,2,128]{2,1,0:T(2,128)S(1)}, f32[2,2,128]{2,1,0:T(2,128)S(1)}, u32[]{:S(2)}, u32[]{:S(2)}) collective-permute-start(f32[2,2,128]{2,1,0:T(2,128)S(1)} %pad_maximum_fusion.16), channel_id=1, source_target_pairs={{0,16},{8,24},{16,0},{24,8},{1,17},{9,25},{17,1},{25,9},{2,18},{10... | collective-permute-start | bytes 6152 | tf_op jit(solution)/shard_map/ppermute | solution.py:15
  119.6 43.5 %collective-permute-start.3 = (bf16[2,128,2048]{2,1,0:T(8,128)(2,1)}, bf16[2,128,2048]{2,1,0:T(8,128)(2,1)S(1)}, u32[]{:S(2)}, u32[]{:S(2)}) collective-permute-start(bf16[2,128,2048]{2,1,0:T(8,128)(2,1)} %bitcast.11), channel_id=1, source_target_pairs={{0,16},{8,24},{16,0},{24,8},{1,17},{9,25},{17,1},{25,9},{2,18},{10... | collective-permute-start | bytes 3145736 | tf_op jit(solution)/shard_map/ppermute | solution.py:15
  121.1 36.1 %copy-start = (bf16[2,4096,128]{1,2,0:T(8,128)(2,1)S(1)}, bf16[2,4096,128]{1,2,0:T(8,128)(2,1)}, u32[]{:S(2)}) copy-start(bf16[2,4096,128]{1,2,0:T(8,128)(2,1)} %copy.40) | copy-start | bytes 6291460
  121.9 47.3 %copy-start.4 = (bf16[256,2048]{1,0:T(8,128)(2,1)}, bf16[256,2048]{1,0:T(8,128)(2,1)S(1)}, u32[]{:S(2)}) copy-start(bf16[256,2048]{1,0:T(8,128)(2,1)S(1)} %convolution_convert_fusion.10) | copy-start | bytes 3145732
  121.9 39.5 %copy-start.5 = (bf16[2,256,4096]{2,1,0:T(8,128)(2,1)S(1)}, bf16[2,256,4096]{2,1,0:T(8,128)(2,1)}, u32[]{:S(2)}) copy-start(bf16[2,256,4096]{2,1,0:T(8,128)(2,1)} %constant_dynamic-update-slice_fusion.1) | copy-start | bytes 12582916
  121.9 44.3 %collective-permute-start.1 = (bf16[2,128,2048]{2,1,0:T(8,128)(2,1)S(1)}, bf16[2,128,2048]{2,1,0:T(8,128)(2,1)S(1)}, u32[]{:S(2)}, u32[]{:S(2)}) collective-permute-start(bf16[2,128,2048]{2,1,0:T(8,128)(2,1)S(1)} %bitcast.50), channel_id=1, source_target_pairs={{0,16},{8,24},{16,0},{24,8},{1,17},{9,25},{17,1},{25,9},{2,18},{10... | collective-permute-start | bytes 3145736 | tf_op jit(solution)/shard_map/ppermute | solution.py:15
  163.2 4.0 %copy-start.10 = (bf16[2,128,2048]{2,1,0:T(8,128)(2,1)}, bf16[2,128,2048]{2,1,0:T(8,128)(2,1)S(1)}, u32[]{:S(2)}) copy-start(bf16[2,128,2048]{2,1,0:T(8,128)(2,1)S(1)} %collective-permute-done.3) | copy-start | bytes 3145732
  166.3 2.9 copy-start.12
  167.2 71.7 %copy-start.13 = (bf16[2,256,256]{1,2,0:T(8,128)(2,1)}, bf16[2,256,256]{1,2,0:T(8,128)(2,1)S(1)}, u32[]{:S(2)}) copy-start(bf16[2,256,256]{1,2,0:T(8,128)(2,1)S(1)} %get-tuple-element.24) | copy-start | bytes 786436
  173.1 23.9 %collective-permute-start.6 = (bf16[2,128,2048]{2,1,0:T(8,128)(2,1)S(1)}, bf16[2,128,2048]{2,1,0:T(8,128)(2,1)S(1)}, u32[]{:S(2)}, u32[]{:S(2)}) collective-permute-start(bf16[2,128,2048]{2,1,0:T(8,128)(2,1)S(1)} %convolution_convert_fusion.8), channel_id=1, source_target_pairs={{0,16},{8,24},{16,0},{24,8},{1,17},{9,25},{17,1},{25,9},{2,18},{10... | collective-permute-start | bytes 3145736 | tf_op jit(solution)/shard_map/ppermute | solution.py:15
  200.7 53.0 %all-to-all-start.2 = ((bf16[8,48,2048]{2,1,0:T(8,128)(2,1)}), bf16[8,48,2048]{2,1,0:T(8,128)(2,1)S(1)}, u32[]{:S(2)}, u32[]{:S(2)}) async-start(bf16[8,48,2048]{2,1,0:T(8,128)(2,1)} %bitcast.14), calls=%async_computation.2 | async-start | bytes 3145728 | tf_op jit(solution)/shard_map/all_to_all | solution.py:20
  205.3 3.6 %copy-start.8 = (bf16[1,2,128,4096]{3,2,1,0:T(8,128)(2,1)S(1)}, bf16[1,2,128,4096]{3,2,1,0:T(8,128)(2,1)}, u32[]{:S(2)}) copy-start(bf16[1,2,128,4096]{3,2,1,0:T(8,128)(2,1)} %param.11) | copy-start | bytes 6291460
  205.3 48.4 %collective-permute-start.8 = (bf16[2,128,4096]{2,1,0:T(8,128)(2,1)}, bf16[2,128,4096]{2,1,0:T(8,128)(2,1)}, u32[]{:S(2)}, u32[]{:S(2)}) collective-permute-start(bf16[2,128,4096]{2,1,0:T(8,128)(2,1)} %pad_maximum_fusion.5), channel_id=1, source_target_pairs={{0,8},{8,0},{16,24},{24,16},{1,9},{9,1},{17,25},{25,17},{2,10},{10... | collective-permute-start | bytes 6291464 | tf_op jit(solution)/shard_map/ppermute | solution.py:15
  208.9 30.1 %copy-start.1 = (bf16[2,4096,128]{1,2,0:T(8,128)(2,1)S(1)}, bf16[2,4096,128]{1,2,0:T(8,128)(2,1)}, u32[]{:S(2)}) copy-start(bf16[2,4096,128]{1,2,0:T(8,128)(2,1)} %copy.40) | copy-start | bytes 6291460
  213.7 25.2 %collective-permute-start.7 = (bf16[2,128,2048]{2,1,0:T(8,128)(2,1)S(1)}, bf16[2,128,2048]{2,1,0:T(8,128)(2,1)S(1)}, u32[]{:S(2)}, u32[]{:S(2)}) collective-permute-start(bf16[2,128,2048]{2,1,0:T(8,128)(2,1)S(1)} %convolution_convert_fusion.5), channel_id=1, source_target_pairs={{0,16},{8,24},{16,0},{24,8},{1,17},{9,25},{17,1},{25,9},{2,18},{10... | collective-permute-start | bytes 3145736 | tf_op jit(solution)/shard_map/ppermute | solution.py:15
  253.6 53.1 %all-to-all-start.3 = ((bf16[8,48,2048]{2,1,0:T(8,128)(2,1)}), bf16[8,48,2048]{2,1,0:T(8,128)(2,1)S(1)}, u32[]{:S(2)}, u32[]{:S(2)}) async-start(bf16[8,48,2048]{2,1,0:T(8,128)(2,1)} %bitcast.17), calls=%async_computation.3 | async-start | bytes 3145728 | tf_op jit(solution)/shard_map/all_to_all | solution.py:20
  258.4 48.4 %collective-permute-start.9 = (bf16[2,4096,128]{2,1,0:T(8,128)(2,1)}, bf16[2,4096,128]{2,1,0:T(8,128)(2,1)}, u32[]{:S(2)}, u32[]{:S(2)}) collective-permute-start(bf16[2,4096,128]{2,1,0:T(8,128)(2,1)} %convolution_convert_fusion), channel_id=1, source_target_pairs={{0,8},{8,0},{16,24},{24,16},{1,9},{9,1},{17,25},{25,17},{2,10},{10... | collective-permute-start | bytes 6291464 | tf_op jit(solution)/shard_map/ppermute | solution.py:15
  259.9 3.8 %copy-start.11 = (bf16[2,128,2048]{2,1,0:T(8,128)(2,1)S(1)}, bf16[2,128,2048]{2,1,0:T(8,128)(2,1)}, u32[]{:S(2)}) copy-start(bf16[2,128,2048]{2,1,0:T(8,128)(2,1)} %copy-done.10) | copy-start | bytes 3145732
  259.9 5.6 %collective-permute-start.10 = (f32[2,128]{1,0:T(2,128)S(1)}, f32[2,128]{1,0:T(2,128)S(1)}, u32[]{:S(2)}, u32[]{:S(2)}) collective-permute-start(f32[2,128]{1,0:T(2,128)S(1)} %slice.83), channel_id=1, source_target_pairs={{0,16},{8,24},{16,0},{24,8},{1,17},{9,25},{17,1},{25,9},{2,18},{10... | collective-permute-start | bytes 3080 | tf_op jit(solution)/shard_map/ppermute | solution.py:15
  271.0 36.3 %copy-start.2 = (bf16[128,2048]{1,0:T(8,128)(2,1)S(1)}, bf16[128,2048]{1,0:T(8,128)(2,1)}, u32[]{:S(2)}) copy-start(bf16[128,2048]{1,0:T(8,128)(2,1)} %convolution_convert_fusion.12) | copy-start | bytes 1572868
  306.7 1.6 copy-start.9
  306.7 1.7 copy-start.14

commit v3 on v2

--- a/solution.py
+++ b/solution.py
@@ -70,12 +70,17 @@
     part = width // PARTS
     columns = [slice(k * part, (k + 1) * part) for k in range(PARTS)]
     upstream = []
-    for cols in columns:
+    for k, cols in enumerate(columns):
         sent = jnp.dot(send_pick, out_grad[0][:, cols], preferred_element_type=F32).astype(BF16)
+        if k == 1:
+            sent, x_other, w_in_other = lax.optimization_barrier((sent, x_other, w_in_other))
         got = exchange(sent, owners)
         grad_own = jnp.dot(slot_pick, got, preferred_element_type=F32).astype(BF16)
         grad_own = grad_own.reshape(experts, cap, part)
-        upstream.append(jnp.concatenate([grad_own, swap(grad_own, 2)], axis=1))
+        grad_other = swap(grad_own, 2)
+        if k == PARTS - 1:
+            grad_other, other_scalars = lax.optimization_barrier((grad_other, other_scalars))
+        upstream.append(jnp.concatenate([grad_own, grad_other], axis=1))
 
     inputs = jnp.concatenate([x_own, x_other], axis=1)
     proj_in = jnp.concatenate([w_in, w_in_other], axis=2)
@@ -104,38 +109,25 @@
     def grad_in(units):
         return jnp.einsum("ecd,ecf->edf", inputs, units, preferred_element_type=F32)
 
-    back_got = []
-    for k, cols in enumerate(columns):
-        back_other = jnp.einsum(
-            "ecf,edf->ecd", pre_grad[:, cap:], proj_in[:, cols], preferred_element_type=F32
-        ).astype(BF16)
-        if k == 0:
-            grad_out_other = grad_out(hidden[..., quarter:]).astype(BF16)
-            back_other, grad_out_other = lax.optimization_barrier((back_other, grad_out_other))
-            grad_out_got = swap(grad_out_other, 1)
-        if k == PARTS - 1:
-            grad_in_other = grad_in(pre_grad[..., quarter:]).astype(BF16)
-            back_other, grad_in_other = lax.optimization_barrier((back_other, grad_in_other))
-            grad_in_got = swap(grad_in_other, 1)
-        back_got.append(swap(back_other, 2))
+    grad_out_other = grad_out(hidden[..., quarter:]).astype(BF16)
+    back_other = jnp.einsum(
+        "ecf,edf->ecd", pre_grad[:, cap:], proj_in, preferred_element_type=F32
+    ).astype(BF16)
+    back_other, grad_out_other = lax.optimization_barrier((back_other, grad_out_other))
+    grad_out_got = swap(grad_out_other, 1)
+    back_got = swap(back_other, 2)
+    grad_in_got = swap(grad_in(pre_grad[..., quarter:]).astype(BF16), 1)
 
-    returned = []
-    for k, cols in enumerate(columns):
-        back_own = jnp.einsum(
-            "ecf,edf->ecd", pre_grad[:, :cap], proj_in[:, cols], preferred_element_type=F32
-        )
-        slot_back = (back_own + back_got[k].astype(F32)).astype(BF16).reshape(slots, part)
-        outgoing = jnp.dot(slot_pick.T, slot_back, preferred_element_type=F32).astype(BF16)
-        if k == PARTS - 1:
-            outgoing, grad_out_got = lax.optimization_barrier((outgoing, grad_out_got))
-        returned.append(exchange(outgoing, owners))
+    back_own = jnp.einsum("ecf,edf->ecd", pre_grad[:, :cap], proj_in, preferred_element_type=F32)
+    slot_back = (back_own + back_got.astype(F32)).astype(BF16).reshape(slots, width)
+    outgoing = jnp.dot(slot_pick.T, slot_back, preferred_element_type=F32).astype(BF16)
+    outgoing, grad_out_got = lax.optimization_barrier((outgoing, grad_out_got))
+    returned = exchange(outgoing, owners)
 
     w_out_grad = (grad_out(hidden[..., :quarter]) + grad_out_got.astype(F32)).astype(BF16)
-    returned[-1], grad_in_got = lax.optimization_barrier((returned[-1], grad_in_got))
+    returned, grad_in_got = lax.optimization_barrier((returned, grad_in_got))
     w_in_grad = (grad_in(pre_grad[..., :quarter]) + grad_in_got.astype(F32)).astype(BF16)
-    token_grad = jnp.concatenate(
-        [jnp.dot(send_pick.T, r, preferred_element_type=F32).astype(BF16) for r in returned], axis=1
-    )
+    token_grad = jnp.dot(send_pick.T, returned, preferred_element_type=F32).astype(BF16)
     gate_grad = gate_part[:, :cap] + gate_got
     return token_grad[None], gate_grad[None], w_in_grad, w_out_grad
 

time: 315 us -> 311 us (0.987)
  waiting for transfers between devices: 206 us -> 213 us
  other arithmetic: 7.96 us -> 3.24 us
  starting transfers between devices: 30.6 us -> 26.1 us
    all_to_all x4 -> x3, waiting for transfers between devices: 36 us -> 81.5 us  [exchange(): lax.all_to_all(blocks, 'expert', split_axis=0, concat_axis=0, tiled=True)]
    ppermute x11 -> x10, waiting for transfers between devices: 170 us -> 132 us  [swap(): return lax.ppermute(value, 'dp', [(i, i ^ bit) for i in range(size)])]
    all_to_all x4 -> x3, starting transfers between devices: 16.6 us -> 13 us  [exchange(): lax.all_to_all(blocks, 'expert', split_axis=0, concat_axis=0, tiled=True)]
    dot_general x6 -> x3, matrix products: 9.13 us -> 6.62 us  [the longest x1 2.47 us: shards(): jnp.einsum('ecf,edf->ecd', pre_grad[:, :cap], proj_in, preferred_element_...]
    ppermute x11 -> x10, starting transfers between devices: 14 us -> 13.1 us  [swap(): return lax.ppermute(value, 'dp', [(i, i ^ bit) for i in range(size)])]
    unnamed x34 -> x32, local copies, waits for them, and re-layouts: 7.37 us -> 7.61 us
  transfers between devices with their start and end apart: 15 -> 13, of which waited for: 8 -> 8; matrix products, arithmetic and copies ran while one was open for 13% -> 12% of each run, Pallas kernels for 0% -> 0%
where the time goes in v3:
time: 311 us; the launch traced here: 310 us
  waiting for transfers between devices  213 us (68%)
  matrix products  42.7 us (14%)
  starting transfers between devices  26.1 us (8%)
  blocking collectives  12.9 us (4%)
  local copies, waits for them, and re-layouts  10.9 us (4%)
  other arithmetic  3.24 us (1%)
    ppermute x10, waiting for transfers between devices, swap(): return lax.ppermute(value, 'dp', [(i, i ^ bit) for i in range(size)])  132 us
    all_to_all x3, waiting for transfers between devices, exchange(): lax.all_to_all(blocks, 'expert', split_axis=0, concat_axis=0, tiled=True)  81.5 us
    ppermute x10, starting transfers between devices, swap(): return lax.ppermute(value, 'dp', [(i, i ^ bit) for i in range(size)])  13.1 us
    all_to_all x3, starting transfers between devices, exchange(): lax.all_to_all(blocks, 'expert', split_axis=0, concat_axis=0, tiled=True)  13 us
    all_gather x1, blocking collectives, shards(): lax.all_gather(jnp.concatenate([tokens, count[0]]), 'expert', axis=0)  12.9 us
    dot_general x2, matrix products, grad_in(): return jnp.einsum('ecd,ecf->edf', inputs, units, preferred_element_type=F32)  9.99 us
    unnamed x32, local copies, waits for them, and re-layouts  7.61 us
  transfers between devices with their start and end apart: 13, of which 8 were waited for; matrix products, arithmetic and copies ran while one was open for 12% of the time, Pallas kernels for 0%

profile of v3, /device:TPU:0, one launch (start us, length us, event | category | flops | bytes accessed | tf_op | source)
XLA Modules:
  0.0 310.0 jit_solution(8111326528220541646)
XLA Ops:
  0.7 3.0 copy.31
  3.7 3.0 collective-permute-start.1
  8.2 12.9 %all-gather.1 = s32[8,1,384]{2,1,0:T(1,128)S(1)} all-gather(s32[1,1,384]{2,1,0:T(1,128)S(1)} %reshape.142), channel_id=2, replica_groups=mesh['dp'=4,'expert'=8] {'expert'}, dimensions={0}, use_global_device_ids=true | all-gather | bytes 13824 | tf_op jit(solution)/shard_map/all_gather | solution.py:46
  21.7 1.8 convolution_convert_fusion.5
  23.4 29.0 %collective-permute-done.1 = bf16[2,4096,128]{1,2,0:T(8,128)(2,1)} collective-permute-done((bf16[2,4096,128]{1,2,0:T(8,128)(2,1)S(1)}, bf16[2,4096,128]{1,2,0:T(8,128)(2,1)}, u32[]{:S(2)}, u32[]{:S(2)}) %collective-permute-start.1) | collective-permute-done | bytes 2097184 | tf_op jit(solution)/shard_map/ppermute | solution.py:15
  52.4 1.7 collective-permute-done
  54.1 4.9 %all-to-all-start = ((bf16[8,48,2048]{2,1,0:T(8,128)(2,1)}), bf16[8,48,2048]{2,1,0:T(8,128)(2,1)}, u32[]{:S(2)}, u32[]{:S(2)}) async-start(bf16[8,48,2048]{2,1,0:T(8,128)(2,1)} %bitcast.43), calls=%async_computation | async-start | bytes 3145728 | tf_op jit(solution)/shard_map/all_to_all | solution.py:20
  59.6 1.8 convolution_convert_fusion.4
  61.3 35.6 %all-to-all-done = bf16[8,48,2048]{2,1,0:T(8,128)(2,1)} async-done(((bf16[8,48,2048]{2,1,0:T(8,128)(2,1)}), bf16[8,48,2048]{2,1,0:T(8,128)(2,1)}, u32[]{:S(2)}, u32[]{:S(2)}) %all-to-all-start) | async-done | bytes 1572896 | tf_op jit(solution)/shard_map/all_to_all | solution.py:20
  96.9 4.3 %all-to-all-start.1 = ((bf16[8,48,2048]{2,1,0:T(8,128)(2,1)}), bf16[8,48,2048]{2,1,0:T(8,128)(2,1)}, u32[]{:S(2)}, u32[]{:S(2)}) async-start(bf16[8,48,2048]{2,1,0:T(8,128)(2,1)} %bitcast.42), calls=%async_computation.1 | async-start | bytes 3145728 | tf_op jit(solution)/shard_map/all_to_all | solution.py:20
  103.4 3.1 %constant_dynamic-update-slice_fusion.1 = bf16[2,256,4096]{2,1,0:T(8,128)(2,1)} fusion(bf16[2,128,4096]{2,1,0:T(8,128)(2,1)} %param.13), kind=kLoop, calls=%fused_computation.84 | loop fusion | bytes 4194304
  106.5 2.2 convolution_convert_fusion.9
  109.2 3.2 %constant_dynamic-update-slice_fusion = bf16[2,256,4096]{2,1,0:T(8,128)(2,1)} fusion(bf16[2,256,4096]{2,1,0:T(8,128)(2,1)} %constant_dynamic-update-slice_fusion.1, bf16[2,128,4096]{2,1,0:T(8,128)(2,1)} %collective-permute-done.5), kind=kLoop, calls=%fused_computation.83 | loop fusion | bytes 4194304 | tf_op jit(solution)/shard_map/concatenate | solution.py:87
  112.4 26.7 %all-to-all-done.1 = bf16[8,48,2048]{2,1,0:T(8,128)(2,1)} async-done(((bf16[8,48,2048]{2,1,0:T(8,128)(2,1)}), bf16[8,48,2048]{2,1,0:T(8,128)(2,1)}, u32[]{:S(2)}, u32[]{:S(2)}) %all-to-all-start.1) | async-done | bytes 1572896 | tf_op jit(solution)/shard_map/all_to_all | solution.py:20
  139.1 2.2 convolution_convert_fusion.8
  142.8 4.1 %fusion.12 = f32[2,256,256]{1,2,0:T(8,128)S(1)} fusion(bf16[2,4096,128]{1,2,0:T(8,128)(2,1)} %collective-permute-done.1, bf16[2,4096,128]{1,2,0:T(8,128)(2,1)S(1)} %copy.31, bf16[2,128,4096]{2,1,0:T(8,128)(2,1)} %collective-permute-done, bf16[2,128,4096]{2,1,0:T(8,128)(2,1)} %bitcast.61), kind=kOutput, calls=%fused_computation.30 | convolution fusion | flops 1090519040 | bytes 8912896 | tf_op jit(solution)/shard_map/ecd,edf->ecf/dot_general | solution.py:90
  147.0 2.7 fusion.2
  149.7 16.3 %collective-permute-done.4 = bf16[2,128,2048]{2,1,0:T(8,128)(2,1)S(1)} collective-permute-done((bf16[2,128,2048]{2,1,0:T(8,128)(2,1)S(1)}, bf16[2,128,2048]{2,1,0:T(8,128)(2,1)S(1)}, u32[]{:S(2)}, u32[]{:S(2)}) %collective-permute-start.4) | collective-permute-done | bytes 1048608 | tf_op jit(solution)/shard_map/ppermute | solution.py:15
  166.0 2.9 multiply_reduce_fusion
  168.9 2.0 convolution_convert_fusion.6
  170.9 2.4 convolution_convert_fusion.2
  176.3 44.2 %collective-permute-done.6 = bf16[2,128,4096]{2,1,0:T(8,128)(2,1)S(1)} collective-permute-done((bf16[2,128,4096]{2,1,0:T(8,128)(2,1)S(1)}, bf16[2,128,4096]{2,1,0:T(8,128)(2,1)S(1)}, u32[]{:S(2)}, u32[]{:S(2)}) %collective-permute-start.6) | collective-permute-done | bytes 2097184 | tf_op jit(solution)/shard_map/ppermute | solution.py:15
  220.6 2.5 add_convert_fusion.1
  223.0 2.8 convolution_convert_fusion
  227.1 3.8 %all-to-all-start.2 = ((bf16[8,48,4096]{2,1,0:T(8,128)(2,1)}), bf16[8,48,4096]{2,1,0:T(8,128)(2,1)S(1)}, u32[]{:S(2)}, u32[]{:S(2)}) async-start(bf16[8,48,4096]{2,1,0:T(8,128)(2,1)} %bitcast.41), calls=%async_computation.2 | async-start | bytes 6291456 | tf_op jit(solution)/shard_map/all_to_all | solution.py:20
  231.0 4.1 %convolution_convert_fusion.1 = bf16[2,4096,128]{2,1,0:T(8,128)(2,1)S(1)} fusion(bf16[2,128,4096]{2,1,0:T(8,128)(2,1)} %collective-permute-done, bf16[2,128,4096]{2,1,0:T(8,128)(2,1)} %bitcast.62, bf16[2,256,256]{1,2,0:T(8,128)(2,1)S(1)} %get-tuple-element.30), kind=kOutput, calls=%fused_computation.1 | convolution fusion | flops 546308096 | bytes 6422528 | tf_op jit(solution)/shard_map/ecd,ecf->edf/dot_general | solution.py:110
  237.2 1.8 fusion.7
  240.7 1.9 fusion.1
  242.6 40.4 %collective-permute-done.8 = bf16[2,4096,128]{2,1,0:T(8,128)(2,1)} collective-permute-done((bf16[2,4096,128]{2,1,0:T(8,128)(2,1)S(1)}, bf16[2,4096,128]{2,1,0:T(8,128)(2,1)}, u32[]{:S(2)}, u32[]{:S(2)}) %collective-permute-start.8) | collective-permute-done | bytes 2097184 | tf_op jit(solution)/shard_map/ppermute | solution.py:15
  283.0 19.2 %all-to-all-done.2 = bf16[8,48,4096]{2,1,0:T(8,128)(2,1)S(1)} async-done(((bf16[8,48,4096]{2,1,0:T(8,128)(2,1)}), bf16[8,48,4096]{2,1,0:T(8,128)(2,1)S(1)}, u32[]{:S(2)}, u32[]{:S(2)}) %all-to-all-start.2) | async-done | bytes 3145760 | tf_op jit(solution)/shard_map/all_to_all | solution.py:20
  302.2 5.9 %add_convert_fusion = bf16[2,4096,128]{2,1,0:T(8,128)(2,1)} fusion(bf16[2,4096,128]{2,1,0:T(8,128)(2,1)} %collective-permute-done.8, bf16[2,128,4096]{2,1,0:T(8,128)(2,1)} %collective-permute-done, bf16[2,128,4096]{2,1,0:T(8,128)(2,1)} %bitcast.63, bf16[2,256,256]{1,2,0:T(8,128)(2,1)S(1)} %get-tuple-element.30), kind=kOutput, calls=%fused_computation.9 | convolution fusion | flops 548405248 | bytes 8519680 | tf_op jit(solution)/shard_map/ecd,ecf->edf/dot_general | solution.py:110
  308.2 1.8 fusion
  (66 shorter events, 14.9 us)
Async XLA Ops:
  0.6 7.6 %copy-start.7 = (s32[1,2,128]{2,1,0:T(2,128)S(1)}, s32[1,2,128]{2,1,0:T(2,128)}, u32[]{:S(2)}) copy-start(s32[1,2,128]{2,1,0:T(2,128)} %param.9) | copy-start | bytes 3076
  0.6 7.6 %copy-start.9 = (s32[1,128]{1,0:T(1,128)S(1)}, s32[1,128]{1,0:T(1,128)}, u32[]{:S(2)}) copy-start(s32[1,128]{1,0:T(1,128)} %param.8) | copy-start | bytes 1540
  0.7 21.0 %copy-start.2 = (bf16[1,128,4096]{2,1,0:T(8,128)(2,1)S(1)}, bf16[1,128,4096]{2,1,0:T(8,128)(2,1)}, u32[]{:S(2)}) copy-start(bf16[1,128,4096]{2,1,0:T(8,128)(2,1)} %param.7) | copy-start | bytes 3145732
  3.7 48.7 %collective-permute-start.1 = (bf16[2,4096,128]{1,2,0:T(8,128)(2,1)S(1)}, bf16[2,4096,128]{1,2,0:T(8,128)(2,1)}, u32[]{:S(2)}, u32[]{:S(2)}) collective-permute-start(bf16[2,4096,128]{1,2,0:T(8,128)(2,1)S(1)} %copy.31), channel_id=1, source_target_pairs={{0,8},{8,0},{16,24},{24,16},{1,9},{9,1},{17,25},{25,17},{2,10},{10... | collective-permute-start | bytes 6291464 | tf_op jit(solution)/shard_map/ppermute | solution.py:15
  6.7 47.4 %collective-permute-start = (bf16[2,128,4096]{2,1,0:T(8,128)(2,1)}, bf16[2,128,4096]{2,1,0:T(8,128)(2,1)}, u32[]{:S(2)}, u32[]{:S(2)}) collective-permute-start(bf16[2,128,4096]{2,1,0:T(8,128)(2,1)} %bitcast.60), channel_id=1, source_target_pairs={{0,16},{8,24},{16,0},{24,8},{1,17},{9,25},{17,1},{25,9},{2,18},{10... | collective-permute-start | bytes 6291464 | tf_op jit(solution)/shard_map/ppermute | solution.py:15
  54.1 42.8 %all-to-all-start = ((bf16[8,48,2048]{2,1,0:T(8,128)(2,1)}), bf16[8,48,2048]{2,1,0:T(8,128)(2,1)}, u32[]{:S(2)}, u32[]{:S(2)}) async-start(bf16[8,48,2048]{2,1,0:T(8,128)(2,1)} %bitcast.43), calls=%async_computation | async-start | bytes 3145728 | tf_op jit(solution)/shard_map/all_to_all | solution.py:20
  59.0 42.6 %copy-start.8 = (f32[1,2,128]{2,1,0:T(2,128)S(1)}, f32[1,2,128]{2,1,0:T(2,128)}, u32[]{:S(2)}) copy-start(f32[1,2,128]{2,1,0:T(2,128)} %param.10) | copy-start | bytes 3076
  59.0 50.3 %collective-permute-start.5 = (bf16[2,128,4096]{2,1,0:T(8,128)(2,1)}, bf16[2,128,4096]{2,1,0:T(8,128)(2,1)}, u32[]{:S(2)}, u32[]{:S(2)}) collective-permute-start(bf16[2,128,4096]{2,1,0:T(8,128)(2,1)} %param.13), channel_id=1, source_target_pairs={{0,8},{8,0},{16,24},{24,16},{1,9},{9,1},{17,25},{25,17},{2,10},{10... | collective-permute-start | bytes 6291464 | tf_op jit(solution)/shard_map/ppermute | solution.py:15
  96.9 42.2 %all-to-all-start.1 = ((bf16[8,48,2048]{2,1,0:T(8,128)(2,1)}), bf16[8,48,2048]{2,1,0:T(8,128)(2,1)}, u32[]{:S(2)}, u32[]{:S(2)}) async-start(bf16[8,48,2048]{2,1,0:T(8,128)(2,1)} %bitcast.42), calls=%async_computation.1 | async-start | bytes 3145728 | tf_op jit(solution)/shard_map/all_to_all | solution.py:20
  101.6 45.4 %collective-permute-start.3 = (f32[2,2,128]{2,1,0:T(2,128)S(1)}, f32[2,2,128]{2,1,0:T(2,128)S(1)}, u32[]{:S(2)}, u32[]{:S(2)}) collective-permute-start(f32[2,2,128]{2,1,0:T(2,128)S(1)} %pad_maximum_fusion.22), channel_id=1, source_target_pairs={{0,16},{8,24},{16,0},{24,8},{1,17},{9,25},{17,1},{25,9},{2,18},{10... | collective-permute-start | bytes 6152 | tf_op jit(solution)/shard_map/ppermute | solution.py:15
  108.7 60.3 %copy-start.3 = (bf16[256,2048]{1,0:T(8,128)(2,1)}, bf16[256,2048]{1,0:T(8,128)(2,1)S(1)}, u32[]{:S(2)}) copy-start(bf16[256,2048]{1,0:T(8,128)(2,1)S(1)} %convolution_convert_fusion.9) | copy-start | bytes 3145732
  108.7 38.3 %collective-permute-start.2 = (bf16[2,128,2048]{2,1,0:T(8,128)(2,1)S(1)}, bf16[2,128,2048]{2,1,0:T(8,128)(2,1)}, u32[]{:S(2)}, u32[]{:S(2)}) collective-permute-start(bf16[2,128,2048]{2,1,0:T(8,128)(2,1)S(1)} %bitcast.46), channel_id=1, source_target_pairs={{0,16},{8,24},{16,0},{24,8},{1,17},{9,25},{17,1},{25,9},{2,18},{10... | collective-permute-start | bytes 3145736 | tf_op jit(solution)/shard_map/ppermute | solution.py:15
  141.2 32.1 %copy-start.5 = (bf16[256,2048]{1,0:T(8,128)(2,1)}, bf16[256,2048]{1,0:T(8,128)(2,1)S(1)}, u32[]{:S(2)}) copy-start(bf16[256,2048]{1,0:T(8,128)(2,1)S(1)} %convolution_convert_fusion.8) | copy-start | bytes 3145732
  141.2 24.8 %collective-permute-start.4 = (bf16[2,128,2048]{2,1,0:T(8,128)(2,1)S(1)}, bf16[2,128,2048]{2,1,0:T(8,128)(2,1)S(1)}, u32[]{:S(2)}, u32[]{:S(2)}) collective-permute-start(bf16[2,128,2048]{2,1,0:T(8,128)(2,1)S(1)} %bitcast.50), channel_id=1, source_target_pairs={{0,16},{8,24},{16,0},{24,8},{1,17},{9,25},{17,1},{25,9},{2,18},{10... | collective-permute-start | bytes 3145736 | tf_op jit(solution)/shard_map/ppermute | solution.py:15
  166.0 7.3 %copy-start.10 = (bf16[2,128,2048]{2,1,0:T(8,128)(2,1)}, bf16[2,128,2048]{2,1,0:T(8,128)(2,1)S(1)}, u32[]{:S(2)}) copy-start(bf16[2,128,2048]{2,1,0:T(8,128)(2,1)S(1)} %collective-permute-done.4) | copy-start | bytes 3145732
  168.9 4.4 %copy-start.12 = (bf16[2,256,256]{1,2,0:T(8,128)(2,1)}, bf16[2,256,256]{1,2,0:T(8,128)(2,1)S(1)}, u32[]{:S(2)}) copy-start(bf16[2,256,256]{1,2,0:T(8,128)(2,1)S(1)} %get-tuple-element.27) | copy-start | bytes 786436
  174.2 46.3 %collective-permute-start.6 = (bf16[2,128,4096]{2,1,0:T(8,128)(2,1)S(1)}, bf16[2,128,4096]{2,1,0:T(8,128)(2,1)S(1)}, u32[]{:S(2)}, u32[]{:S(2)}) collective-permute-start(bf16[2,128,4096]{2,1,0:T(8,128)(2,1)S(1)} %convolution_convert_fusion.2), channel_id=1, source_target_pairs={{0,16},{8,24},{16,0},{24,8},{1,17},{9,25},{17,1},{25,9},{2,18},{10... | collective-permute-start | bytes 6291464 | tf_op jit(solution)/shard_map/ppermute | solution.py:15
  175.8 50.0 %collective-permute-start.7 = (bf16[2,128,4096]{2,1,0:T(8,128)(2,1)S(1)}, bf16[2,128,4096]{2,1,0:T(8,128)(2,1)S(1)}, u32[]{:S(2)}, u32[]{:S(2)}) collective-permute-start(bf16[2,128,4096]{2,1,0:T(8,128)(2,1)S(1)} %pad_maximum_fusion.4), channel_id=1, source_target_pairs={{0,8},{8,0},{16,24},{24,16},{1,9},{9,1},{17,25},{25,17},{2,10},{10... | collective-permute-start | bytes 6291464 | tf_op jit(solution)/shard_map/ppermute | solution.py:15
  225.8 1.3 copy-start
  227.1 75.1 %all-to-all-start.2 = ((bf16[8,48,4096]{2,1,0:T(8,128)(2,1)}), bf16[8,48,4096]{2,1,0:T(8,128)(2,1)S(1)}, u32[]{:S(2)}, u32[]{:S(2)}) async-start(bf16[8,48,4096]{2,1,0:T(8,128)(2,1)} %bitcast.41), calls=%async_computation.2 | async-start | bytes 6291456 | tf_op jit(solution)/shard_map/all_to_all | solution.py:20
  231.0 6.2 %copy-start.4 = (bf16[256,2048]{1,0:T(8,128)(2,1)S(1)}, bf16[256,2048]{1,0:T(8,128)(2,1)}, u32[]{:S(2)}) copy-start(bf16[256,2048]{1,0:T(8,128)(2,1)} %copy-done.3) | copy-start | bytes 3145732
  231.0 6.2 %copy-start.13 = (bf16[2,256,256]{1,2,0:T(8,128)(2,1)S(1)}, bf16[2,256,256]{1,2,0:T(8,128)(2,1)}, u32[]{:S(2)}) copy-start(bf16[2,256,256]{1,2,0:T(8,128)(2,1)} %copy-done.12) | copy-start | bytes 786436
  235.1 4.0 %copy-start.6 = (bf16[256,2048]{1,0:T(8,128)(2,1)S(1)}, bf16[256,2048]{1,0:T(8,128)(2,1)}, u32[]{:S(2)}) copy-start(bf16[256,2048]{1,0:T(8,128)(2,1)} %copy-done.5) | copy-start | bytes 3145732
  235.1 4.0 %copy-start.11 = (bf16[2,128,2048]{2,1,0:T(8,128)(2,1)S(1)}, bf16[2,128,2048]{2,1,0:T(8,128)(2,1)}, u32[]{:S(2)}) copy-start(bf16[2,128,2048]{2,1,0:T(8,128)(2,1)} %copy-done.10) | copy-start | bytes 3145732
  235.1 47.9 %collective-permute-start.8 = (bf16[2,4096,128]{2,1,0:T(8,128)(2,1)S(1)}, bf16[2,4096,128]{2,1,0:T(8,128)(2,1)}, u32[]{:S(2)}, u32[]{:S(2)}) collective-permute-start(bf16[2,4096,128]{2,1,0:T(8,128)(2,1)S(1)} %convolution_convert_fusion.1), channel_id=1, source_target_pairs={{0,8},{8,0},{16,24},{24,16},{1,9},{9,1},{17,25},{25,17},{2,10},{10... | collective-permute-start | bytes 6291464 | tf_op jit(solution)/shard_map/ppermute | solution.py:15
  235.7 4.3 %collective-permute-start.9 = (f32[2,128]{1,0:T(2,128)S(1)}, f32[2,128]{1,0:T(2,128)S(1)}, u32[]{:S(2)}, u32[]{:S(2)}) collective-permute-start(f32[2,128]{1,0:T(2,128)S(1)} %slice.67), channel_id=1, source_target_pairs={{0,16},{8,24},{16,0},{24,8},{1,17},{9,25},{17,1},{25,9},{2,18},{10... | collective-permute-start | bytes 3080 | tf_op jit(solution)/shard_map/ppermute | solution.py:15
  239.1 1.6 copy-start.1
